TPU v7x, 512 devices: a whole 4x4x16 slice. The times are simulated.
512 devices in a mesh: dom: 64 (over y, z), row: 8 (over x, core).
Axes of the slice: x: 4, y: 4, z: 16, core: 2. Of those that a mesh axis runs over, the one named last changes fastest.
Arguments:
- embedding: float32 [32768, 400], P(('dom', 'row')), may hold values from -1.5 to 1.5
- adagrad: float32 [32768], P(('dom', 'row')), may hold values from 0.05 to 1
- relation: bfloat16 [4096, 400], replicated, may hold values from -4.1875 to 4.1875
- offsets: int32 [2], replicated, may hold values from 1 to 63
- counts: int32 [2, 512], P(None, ('dom', 'row')), may hold values from 1 to 2048, 524288 in all within a row
- lhs_index: int32 [2, 1048576], P(None, ('dom', 'row')), may hold values from 0 to 511
- rhs_index: int32 [2, 1048576], P(None, ('dom', 'row')), may hold values from 0 to 511
- rel_ids: int32 [2, 1048576], P(None, ('dom', 'row')), may hold values from 0 to 4095
- neg_index: int32 [2, 64, 128], P(None, 'dom'), may hold values from 0 to 511
Outputs:
- embedding_out: float32 [32768, 400], P(('dom', 'row'))
- adagrad_out: float32 [32768], P(('dom', 'row'))
Inputs may be any that keep to these rules, and one draw needn't show every extreme that they name: In every round some device has all 2048 slots live; the counts of one round add up to 524288.
All inputs are finite; a program needn't handle non-finite values.
Results may differ from a plain program's by a relative error of at most 0.0018.
Values may be sent and summed in bfloat16 or wider, within the bound.
A program may use at most 64 MiB of HBM per device.

v0:
```python
import jax
import jax.numpy as jnp
from jax import lax
from jax.sharding import PartitionSpec as P

ROUNDS = 2


learn_rate = 0.1
edge_block = 512


def passed_along(value, axis, by):
    count = lax.axis_size(axis)
    return lax.ppermute(value, axis, [(i, (i + by) % count) for i in range(count)])


def complex_times(heads, rel_rows):
    half_width = heads.shape[1] // 2
    head_re, head_im = (heads[:, :half_width], heads[:, half_width:])
    rel_re, rel_im = (rel_rows[:, :half_width], rel_rows[:, half_width:])
    return jnp.concatenate(
        [head_re * rel_re - head_im * rel_im, head_re * rel_im + head_im * rel_re], axis=1
    )


def complex_back(grads, rel_rows):
    half_width = grads.shape[1] // 2
    grad_re, grad_im = (grads[:, :half_width], grads[:, half_width:])
    rel_re, rel_im = (rel_rows[:, :half_width], rel_rows[:, half_width:])
    return jnp.concatenate(
        [grad_re * rel_re + grad_im * rel_im, grad_im * rel_re - grad_re * rel_im], axis=1
    )


def block_grads(head_panel, tail_panel, neg_rows, relation, head_ids, tail_ids, rel_list, is_live):
    heads = head_panel[head_ids].astype(jnp.float32)
    tails = tail_panel[tail_ids].astype(jnp.float32)
    rel_rows = relation[rel_list].astype(jnp.float32)
    query = complex_times(heads, rel_rows).astype(jnp.bfloat16)
    query_f = query.astype(jnp.float32)
    positive = jnp.sum(query_f * tails, axis=1)
    negative = lax.dot_general(
        query, neg_rows, (((1,), (1,)), ((), ())), preferred_element_type=jnp.float32
    )
    pos_weight = jnp.where(is_live, -jax.nn.sigmoid(-positive), 0.0)
    neg_weight = jnp.where(
        is_live[:, None], jax.nn.sigmoid(negative) / neg_rows.shape[0], 0.0
    ).astype(jnp.bfloat16)
    query_grad = pos_weight[:, None] * tails + jnp.dot(
        neg_weight, neg_rows, preferred_element_type=jnp.float32
    )
    head_grad = complex_back(query_grad, rel_rows)
    tail_grad = pos_weight[:, None] * query_f
    neg_grad = lax.dot_general(
        neg_weight, query, (((0,), (0,)), ((), ())), preferred_element_type=jnp.float32
    )
    return (head_grad, tail_grad, neg_grad)


def add_by_rows(accum, row_ids, values):
    row_iota = jnp.arange(accum.shape[0], dtype=jnp.int32)
    selector = (row_ids[None, :] == row_iota[:, None]).astype(jnp.float32)
    return accum + jnp.dot(
        selector, values, precision=lax.Precision.HIGHEST, preferred_element_type=jnp.float32
    )


def device_grads(head_panel, tail_panel, neg_ids, relation, edge_lists, live_count):
    head_ids, tail_ids, rel_list = edge_lists
    capacity = head_ids.shape[0]
    block_len = min(edge_block, capacity)
    neg_rows = tail_panel[neg_ids]
    row_total = head_panel.shape[0]
    col_total = head_panel.shape[1]

    def cut_block(values, first):
        return lax.dynamic_slice_in_dim(values, first, block_len)

    def step(block_no, accums):
        head_acc, tail_acc, neg_acc = accums
        first = block_no * block_len
        head_part = cut_block(head_ids, first)
        tail_part = cut_block(tail_ids, first)
        is_live = first + jnp.arange(block_len, dtype=jnp.int32) < live_count
        head_grad, tail_grad, neg_grad = block_grads(
            head_panel,
            tail_panel,
            neg_rows,
            relation,
            head_part,
            tail_part,
            cut_block(rel_list, first),
            is_live,
        )
        return (
            add_by_rows(head_acc, head_part, head_grad),
            add_by_rows(tail_acc, tail_part, tail_grad),
            neg_acc + neg_grad,
        )

    zero_rows = jnp.zeros((row_total, col_total), jnp.float32)
    zero_negs = jnp.zeros((neg_ids.shape[0], col_total), jnp.float32)
    block_count = (live_count + block_len - 1) // block_len
    head_acc, tail_acc, neg_acc = lax.fori_loop(
        0, block_count, step, (zero_rows, zero_rows, zero_negs)
    )
    return (head_acc, tail_acc.at[neg_ids].add(neg_acc))


def hop_forward(shard, offset_now, levels, partitions):
    current = shard
    for bit_level in range(levels):
        arrived = passed_along(current, "dom", partitions - (1 << bit_level))
        current = jnp.where(offset_now // (1 << bit_level) % 2 == 1, arrived, current)
    return current


def hop_back(shard, offset_now, levels):
    current = shard
    for bit_level in range(levels):
        arrived = passed_along(current, "dom", 1 << bit_level)
        current = jnp.where(offset_now // (1 << bit_level) % 2 == 1, arrived, current)
    return current


def body(embedding, adagrad, relation, offsets, counts, lhs_index, rhs_index, rel_ids, neg_index):
    partitions = lax.axis_size("dom")
    levels = partitions.bit_length() - 1
    current = embedding
    squares_sum = adagrad
    for round_index in range(ROUNDS):
        offset_now = offsets[round_index]
        working = current.astype(jnp.bfloat16)
        far_shard = hop_forward(working, offset_now, levels, partitions)
        head_panel, tail_panel = (
            lax.all_gather(working, "row", axis=0, tiled=True),
            lax.all_gather(far_shard, "row", axis=0, tiled=True),
        )
        edge_lists = (lhs_index[round_index], rhs_index[round_index], rel_ids[round_index])
        live_count = counts[round_index, 0]
        head_part, tail_part = device_grads(
            head_panel, tail_panel, neg_index[round_index, 0], relation, edge_lists, live_count
        )
        head_sum, tail_sum = (
            lax.psum_scatter(head_part, "row", scatter_dimension=0, tiled=True),
            lax.psum_scatter(tail_part, "row", scatter_dimension=0, tiled=True),
        )
        gradient = head_sum + hop_back(tail_sum, offset_now, levels)
        squares_sum = squares_sum + jnp.mean(gradient * gradient, axis=1)
        current = current - learn_rate * gradient / jnp.sqrt(squares_sum)[:, None]
    return (current, squares_sum)


def solution(mesh):
    return jax.shard_map(
        body,
        mesh=mesh,
        in_specs=(
            P(("dom", "row"), None),
            P(("dom", "row")),
            P(),
            P(),
            P(None, ("dom", "row")),
            P(None, ("dom", "row")),
            P(None, ("dom", "row")),
            P(None, ("dom", "row")),
            P(None, "dom", None),
        ),
        out_specs=(P(("dom", "row"), None), P(("dom", "row"))),
        check_vma=False,
    )
```

profile of v0, /device:TPU:6, one launch (start us, length us, event | category | flops | bytes accessed | tf_op | source)
XLA Modules:
  0.0 585.5 jit_solution(1572827614093197357)
XLA Ops:
  8.1 13.9 %collective-permute-start = (bf16[64,400]{1,0:T(8,128)(2,1)S(1)}, bf16[64,400]{1,0:T(8,128)(2,1)S(1)}, u32[]{:S(2)}, u32[]{:S(2)}) collective-permute-start(bf16[64,400]{1,0:T(8,128)(2,1)S(1)} %convert_element_type.42), channel_id=1, source_target_pairs={{0,504},{8,0},{16,8},{24,16},{32,24},{40,32},{48,40},{56,48},{64,5... | collective-permute-start | bytes 153608 | tf_op jit(solution)/shard_map/ppermute | solution.py:15
  27.9 3.4 collective-permute-start.1
  34.9 5.8 collective-permute-start.2
  41.9 4.1 collective-permute-done.2
  46.1 6.3 %collective-permute-start.3 = (bf16[64,400]{1,0:T(8,128)(2,1)S(1)}, bf16[64,400]{1,0:T(8,128)(2,1)S(1)}, u32[]{:S(2)}, u32[]{:S(2)}) collective-permute-start(bf16[64,400]{1,0:T(8,128)(2,1)S(1)} %broadcast_select_fusion.16), channel_id=1, source_target_pairs={{0,448},{8,456},{16,464},{24,472},{32,480},{40,488},{48,496},{56,5... | collective-permute-start | bytes 153608 | tf_op jit(solution)/shard_map/ppermute | solution.py:15
  52.4 13.1 %all_gather.12 = bf16[512,400]{1,0:T(8,128)(2,1)S(1)} all-gather(bf16[64,400]{1,0:T(8,128)(2,1)S(1)} %convert_element_type.42), channel_id=1, replica_groups=mesh['dom'=64,'row'=8] {'row'}, dimensions={0}, use_global_device_ids=true | all-gather | bytes 460800 | tf_op jit(solution)/shard_map/all_gather | solution.py:137
  65.5 2.3 collective-permute-start.4
  69.2 2.5 collective-permute-done.4
  71.7 2.3 collective-permute-start.5
  74.7 6.0 %copy.17 = bf16[4096,400]{1,0:T(8,128)(2,1)} copy(bf16[4096,400]{0,1:T(8,128)(2,1)} %param.15) | data formatting | bytes 6553600 | tf_op jit(solution)/shard_map/while | solution.py:105
  80.8 13.1 %all_gather.13 = bf16[512,400]{1,0:T(8,128)(2,1)S(1)} all-gather(bf16[64,400]{1,0:T(8,128)(2,1)S(1)} %broadcast_select_fusion.21), channel_id=1, replica_groups=mesh['dom'=64,'row'=8] {'row'}, dimensions={0}, use_global_device_ids=true | all-gather | bytes 460800 | tf_op jit(solution)/shard_map/all_gather | solution.py:138
  98.1 76.5 %while.28 = (s32[]{:T(128)}, f32[512,400]{0,1:T(8,128)}, f32[512,400]{0,1:T(8,128)}, f32[128,400]{0,1:T(8,128)}, s32[]{:T(128)}, /*index=5*/s32[2048]{0:T(1024)S...) while((s32[]{:T(128)}, f32[512,400]{0,1:T(8,128)}, ...), condition=%wide.region_2.3_spmd, body=%wide.region_0.2_spmd.sunk | while | flops 2682015744 | bytes 27278640 | solution.py:105
  98.9 4.7 gather_fusion.2
  114.3 3.0 convolution_add_fusion.17
  118.0 4.7 gather_fusion.2
  133.4 3.0 convolution_add_fusion.17
  137.1 4.7 gather_fusion.2
  152.5 3.0 convolution_add_fusion.17
  156.2 4.7 gather_fusion.2
  171.6 3.0 convolution_add_fusion.17
  180.1 37.5 %reduce-scatter.7.cloned.1.call-done = f32[64,400]{1,0:T(8,128)} async-done(((f32[512,400]{1,0:T(8,128)}), f32[64,400]{1,0:T(8,128)}) %reduce-scatter.7.cloned.1.call-update) | async-done | bytes 102416 | tf_op jit(solution)/shard_map/reduce_scatter | solution.py:147
  217.5 3.5 collective-permute-start.6
  221.1 2.5 copy.18
  223.6 6.1 %collective-permute-done.6 = f32[64,400]{1,0:T(8,128)S(1)} collective-permute-done((f32[64,400]{1,0:T(8,128)}, f32[64,400]{1,0:T(8,128)S(1)}, u32[]{:S(2)}, u32[]{:S(2)}) %collective-permute-start.6) | collective-permute-done | bytes 102432 | tf_op jit(solution)/shard_map/ppermute | solution.py:15
  232.6 11.0 %collective-permute-done.7 = f32[64,400]{1,0:T(8,128)S(1)} collective-permute-done((f32[64,400]{1,0:T(8,128)S(1)}, f32[64,400]{1,0:T(8,128)S(1)}, u32[]{:S(2)}, u32[]{:S(2)}) %collective-permute-start.7) | collective-permute-done | bytes 102432 | tf_op jit(solution)/shard_map/ppermute | solution.py:15
  243.6 2.8 collective-permute-start.8
  246.4 14.7 %collective-permute-done.8 = f32[64,400]{1,0:T(8,128)S(1)} collective-permute-done((f32[64,400]{1,0:T(8,128)S(1)}, f32[64,400]{1,0:T(8,128)S(1)}, u32[]{:S(2)}, u32[]{:S(2)}) %collective-permute-start.8) | collective-permute-done | bytes 102432 | tf_op jit(solution)/shard_map/ppermute | solution.py:15
  261.1 7.4 %collective-permute-start.9 = (f32[64,400]{1,0:T(8,128)S(1)}, f32[64,400]{1,0:T(8,128)S(1)}, u32[]{:S(2)}, u32[]{:S(2)}) collective-permute-start(f32[64,400]{1,0:T(8,128)S(1)} %broadcast_select_fusion.15), channel_id=1, source_target_pairs={{0,64},{8,72},{16,80},{24,88},{32,96},{40,104},{48,112},{56,120},{... | collective-permute-start | bytes 307208 | tf_op jit(solution)/shard_map/ppermute | solution.py:15
  268.6 13.7 %collective-permute-done.9 = f32[64,400]{1,0:T(8,128)S(1)} collective-permute-done((f32[64,400]{1,0:T(8,128)S(1)}, f32[64,400]{1,0:T(8,128)S(1)}, u32[]{:S(2)}, u32[]{:S(2)}) %collective-permute-start.9) | collective-permute-done | bytes 102432 | tf_op jit(solution)/shard_map/ppermute | solution.py:15
  282.2 2.3 collective-permute-start.10
  284.5 5.9 %collective-permute-done.10 = f32[64,400]{1,0:T(8,128)S(1)} collective-permute-done((f32[64,400]{1,0:T(8,128)S(1)}, f32[64,400]{1,0:T(8,128)S(1)}, u32[]{:S(2)}, u32[]{:S(2)}) %collective-permute-start.10) | collective-permute-done | bytes 102432 | tf_op jit(solution)/shard_map/ppermute | solution.py:15
  292.4 6.4 %collective-permute-done.11 = f32[64,400]{1,0:T(8,128)S(1)} collective-permute-done((f32[64,400]{1,0:T(8,128)S(1)}, f32[64,400]{1,0:T(8,128)S(1)}, u32[]{:S(2)}, u32[]{:S(2)}) %collective-permute-start.11) | collective-permute-done | bytes 102432 | tf_op jit(solution)/shard_map/ppermute | solution.py:15
  304.4 2.3 collective-permute-done.12
  306.7 2.1 collective-permute-start.13
  309.5 4.5 collective-permute-done.13
  313.9 7.6 %collective-permute-start.14 = (bf16[64,400]{1,0:T(8,128)(2,1)S(1)}, bf16[64,400]{1,0:T(8,128)(2,1)S(1)}, u32[]{:S(2)}, u32[]{:S(2)}) collective-permute-start(bf16[64,400]{1,0:T(8,128)(2,1)S(1)} %broadcast_select_fusion.3), channel_id=1, source_target_pairs={{0,480},{8,488},{16,496},{24,504},{32,0},{40,8},{48,16},{56,24},{6... | collective-permute-start | bytes 153608 | tf_op jit(solution)/shard_map/ppermute | solution.py:15
  321.6 3.7 collective-permute-done.14
  325.2 8.9 %collective-permute-start.15 = (bf16[64,400]{1,0:T(8,128)(2,1)S(1)}, bf16[64,400]{1,0:T(8,128)(2,1)S(1)}, u32[]{:S(2)}, u32[]{:S(2)}) collective-permute-start(bf16[64,400]{1,0:T(8,128)(2,1)S(1)} %broadcast_select_fusion.5), channel_id=1, source_target_pairs={{0,448},{8,456},{16,464},{24,472},{32,480},{40,488},{48,496},{56,5... | collective-permute-start | bytes 153608 | tf_op jit(solution)/shard_map/ppermute | solution.py:15
  334.2 5.9 %collective-permute-done.15 = bf16[64,400]{1,0:T(8,128)(2,1)S(1)} collective-permute-done((bf16[64,400]{1,0:T(8,128)(2,1)S(1)}, bf16[64,400]{1,0:T(8,128)(2,1)S(1)}, u32[]{:S(2)}, u32[]{:S(2)}) %collective-permute-start.15) | collective-permute-done | bytes 51232 | tf_op jit(solution)/shard_map/ppermute | solution.py:15
  340.1 4.5 collective-permute-start.16
  346.9 3.4 collective-permute-start.17
  350.3 13.1 %all_gather.14 = bf16[512,400]{1,0:T(8,128)(2,1)S(1)} all-gather(bf16[64,400]{1,0:T(8,128)(2,1)S(1)} %fusion.31), channel_id=1, replica_groups=mesh['dom'=64,'row'=8] {'row'}, dimensions={0}, use_global_device_ids=true | all-gather | bytes 460800 | tf_op jit(solution)/shard_map/all_gather | solution.py:137
  363.4 13.1 %all_gather.15 = bf16[512,400]{1,0:T(8,128)(2,1)S(1)} all-gather(bf16[64,400]{1,0:T(8,128)(2,1)S(1)} %broadcast_select_fusion.10), channel_id=1, replica_groups=mesh['dom'=64,'row'=8] {'row'}, dimensions={0}, use_global_device_ids=true | all-gather | bytes 460800 | tf_op jit(solution)/shard_map/all_gather | solution.py:138
  380.8 73.9 %while.29 = (s32[]{:T(128)}, f32[512,400]{0,1:T(8,128)}, f32[512,400]{0,1:T(8,128)}, f32[128,400]{0,1:T(8,128)}, s32[]{:T(128)}, /*index=5*/s32[2048]{0:T(1024)S...) while((s32[]{:T(128)}, f32[512,400]{0,1:T(8,128)}, ...), condition=%wide.region_9.10_spmd, body=%wide.region_7.9_spmd.sunk | while | flops 2682015744 | bytes 27278640 | solution.py:105
  380.8 4.7 gather_fusion.5
  396.3 3.0 convolution_add_fusion.21
  399.3 4.7 gather_fusion.5
  414.7 3.0 convolution_add_fusion.21
  417.8 4.7 gather_fusion.5
  433.2 3.0 convolution_add_fusion.21
  436.3 4.7 gather_fusion.5
  451.7 3.0 convolution_add_fusion.21
  460.0 35.3 %reduce-scatter.11.cloned.1.call-done = f32[64,400]{1,0:T(8,128)} async-done(((f32[512,400]{1,0:T(8,128)}), f32[64,400]{1,0:T(8,128)}) %reduce-scatter.11.cloned.1.call-update) | async-done | bytes 102416 | tf_op jit(solution)/shard_map/reduce_scatter | solution.py:147
  495.3 3.4 collective-permute-start.18
  498.7 2.5 copy.22
  501.2 6.2 %collective-permute-done.18 = f32[64,400]{1,0:T(8,128)S(1)} collective-permute-done((f32[64,400]{1,0:T(8,128)}, f32[64,400]{1,0:T(8,128)S(1)}, u32[]{:S(2)}, u32[]{:S(2)}) %collective-permute-start.18) | collective-permute-done | bytes 102432 | tf_op jit(solution)/shard_map/ppermute | solution.py:15
  510.2 11.0 %collective-permute-done.19 = f32[64,400]{1,0:T(8,128)S(1)} collective-permute-done((f32[64,400]{1,0:T(8,128)S(1)}, f32[64,400]{1,0:T(8,128)S(1)}, u32[]{:S(2)}, u32[]{:S(2)}) %collective-permute-start.19) | collective-permute-done | bytes 102432 | tf_op jit(solution)/shard_map/ppermute | solution.py:15
  521.3 2.9 collective-permute-start.20
  524.2 14.5 %collective-permute-done.20 = f32[64,400]{1,0:T(8,128)S(1)} collective-permute-done((f32[64,400]{1,0:T(8,128)S(1)}, f32[64,400]{1,0:T(8,128)S(1)}, u32[]{:S(2)}, u32[]{:S(2)}) %collective-permute-start.20) | collective-permute-done | bytes 102432 | tf_op jit(solution)/shard_map/ppermute | solution.py:15
  538.8 7.7 %collective-permute-start.21 = (f32[64,400]{1,0:T(8,128)S(1)}, f32[64,400]{1,0:T(8,128)S(1)}, u32[]{:S(2)}, u32[]{:S(2)}) collective-permute-start(f32[64,400]{1,0:T(8,128)S(1)} %broadcast_select_fusion.4), channel_id=1, source_target_pairs={{0,64},{8,72},{16,80},{24,88},{32,96},{40,104},{48,112},{56,120},{... | collective-permute-start | bytes 307208 | tf_op jit(solution)/shard_map/ppermute | solution.py:15
  546.4 13.6 %collective-permute-done.21 = f32[64,400]{1,0:T(8,128)S(1)} collective-permute-done((f32[64,400]{1,0:T(8,128)S(1)}, f32[64,400]{1,0:T(8,128)S(1)}, u32[]{:S(2)}, u32[]{:S(2)}) %collective-permute-start.21) | collective-permute-done | bytes 102432 | tf_op jit(solution)/shard_map/ppermute | solution.py:15
  562.0 6.3 %collective-permute-done.22 = f32[64,400]{1,0:T(8,128)S(1)} collective-permute-done((f32[64,400]{1,0:T(8,128)S(1)}, f32[64,400]{1,0:T(8,128)S(1)}, u32[]{:S(2)}, u32[]{:S(2)}) %collective-permute-start.22) | collective-permute-done | bytes 102432 | tf_op jit(solution)/shard_map/ppermute | solution.py:15
  568.3 2.5 collective-permute-start.23
  570.8 5.8 collective-permute-done.23
  (300 shorter events, 134.8 us)
Async XLA Ops:
  7.2 210.4 %reduce-scatter.7.cloned.1.call-start = ((), (), s32[]{:S(2)}) async-start(), calls=%async_computation.5 | async-start | bytes 1179648 | tf_op jit(solution)/shard_map/reduce_scatter | solution.py:147
  8.1 18.8 %collective-permute-start = (bf16[64,400]{1,0:T(8,128)(2,1)S(1)}, bf16[64,400]{1,0:T(8,128)(2,1)S(1)}, u32[]{:S(2)}, u32[]{:S(2)}) collective-permute-start(bf16[64,400]{1,0:T(8,128)(2,1)S(1)} %convert_element_type.42), channel_id=1, source_target_pairs={{0,504},{8,0},{16,8},{24,16},{32,24},{40,32},{48,40},{56,48},{64,5... | collective-permute-start | bytes 153608 | tf_op jit(solution)/shard_map/ppermute | solution.py:15
  27.9 7.1 %collective-permute-start.1 = (bf16[64,400]{1,0:T(8,128)(2,1)S(1)}, bf16[64,400]{1,0:T(8,128)(2,1)S(1)}, u32[]{:S(2)}, u32[]{:S(2)}) collective-permute-start(bf16[64,400]{1,0:T(8,128)(2,1)S(1)} %broadcast_select_fusion.12), channel_id=1, source_target_pairs={{0,496},{8,504},{16,0},{24,8},{32,16},{40,24},{48,32},{56,40},{64,... | collective-permute-start | bytes 153608 | tf_op jit(solution)/shard_map/ppermute | solution.py:15
  34.9 11.2 %collective-permute-start.2 = (bf16[64,400]{1,0:T(8,128)(2,1)S(1)}, bf16[64,400]{1,0:T(8,128)(2,1)S(1)}, u32[]{:S(2)}, u32[]{:S(2)}) collective-permute-start(bf16[64,400]{1,0:T(8,128)(2,1)S(1)} %broadcast_select_fusion.14), channel_id=1, source_target_pairs={{0,480},{8,488},{16,496},{24,504},{32,0},{40,8},{48,16},{56,24},{6... | collective-permute-start | bytes 153608 | tf_op jit(solution)/shard_map/ppermute | solution.py:15
  41.9 38.8 %copy-start.13 = (s32[128]{0:T(128)}, s32[128]{0:T(128)S(1)}, u32[]{:S(2)}) copy-start(s32[128]{0:T(128)S(1)} %get-tuple-element.261) | copy-start | bytes 1540
  46.1 19.4 %collective-permute-start.3 = (bf16[64,400]{1,0:T(8,128)(2,1)S(1)}, bf16[64,400]{1,0:T(8,128)(2,1)S(1)}, u32[]{:S(2)}, u32[]{:S(2)}) collective-permute-start(bf16[64,400]{1,0:T(8,128)(2,1)S(1)} %broadcast_select_fusion.16), channel_id=1, source_target_pairs={{0,448},{8,456},{16,464},{24,472},{32,480},{40,488},{48,496},{56,5... | collective-permute-start | bytes 153608 | tf_op jit(solution)/shard_map/ppermute | solution.py:15
  65.5 6.2 %collective-permute-start.4 = (bf16[64,400]{1,0:T(8,128)(2,1)S(1)}, bf16[64,400]{1,0:T(8,128)(2,1)S(1)}, u32[]{:S(2)}, u32[]{:S(2)}) collective-permute-start(bf16[64,400]{1,0:T(8,128)(2,1)S(1)} %broadcast_select_fusion.18), channel_id=1, source_target_pairs={{0,384},{8,392},{16,400},{24,408},{32,416},{40,424},{48,432},{56,4... | collective-permute-start | bytes 153608 | tf_op jit(solution)/shard_map/ppermute | solution.py:15
  71.7 9.0 %collective-permute-start.5 = (bf16[64,400]{1,0:T(8,128)(2,1)S(1)}, bf16[64,400]{1,0:T(8,128)(2,1)S(1)}, u32[]{:S(2)}, u32[]{:S(2)}) collective-permute-start(bf16[64,400]{1,0:T(8,128)(2,1)S(1)} %broadcast_select_fusion.20), channel_id=1, source_target_pairs={{0,256},{8,264},{16,272},{24,280},{32,288},{40,296},{48,304},{56,3... | collective-permute-start | bytes 153608 | tf_op jit(solution)/shard_map/ppermute | solution.py:15
  108.6 4.1 copy-start.2
  108.6 5.1 copy-start.7
  113.8 3.5 copy-start.3
  127.7 4.1 copy-start.2
  127.7 5.1 copy-start.7
  132.9 3.5 copy-start.3
  146.9 4.1 copy-start.2
  146.9 5.1 copy-start.7
  152.0 3.5 copy-start.3
  166.0 4.1 copy-start.2
  166.0 5.1 copy-start.7
  171.1 3.5 copy-start.3
  179.0 1.0 copy-start.4
  179.0 120.9 %copy-start.14 = (f32[64]{0:T(128)S(1)}, f32[64]{0:T(128)}, u32[]{:S(2)}) copy-start(f32[64]{0:T(128)} %param.14) | copy-start | bytes 772
  179.0 120.9 %copy-start.8 = (f32[64,400]{1,0:T(8,128)S(1)}, f32[64,400]{1,0:T(8,128)}, u32[]{:S(2)}) copy-start(f32[64,400]{1,0:T(8,128)} %param.13) | copy-start | bytes 307204
  179.0 165.6 %copy-start.12 = (s32[128]{0:T(128)S(1)}, s32[128]{0:T(128)}, u32[]{:S(2)}) copy-start(s32[128]{0:T(128)} %get-tuple-element.260) | copy-start | bytes 1540
  180.0 112.4 %reduce-scatter.5.cloned.1.call-start = ((), (), s32[]{:S(2)}) async-start(), calls=%async_computation.4 | async-start | bytes 1179648 | tf_op jit(solution)/shard_map/reduce_scatter | solution.py:146
  217.5 12.2 %collective-permute-start.6 = (f32[64,400]{1,0:T(8,128)}, f32[64,400]{1,0:T(8,128)S(1)}, u32[]{:S(2)}, u32[]{:S(2)}) collective-permute-start(f32[64,400]{1,0:T(8,128)} %reduce-scatter.7.cloned.1.call-done), channel_id=1, source_target_pairs={{0,8},{8,16},{16,24},{24,32},{32,40},{40,48},{48,56},{56,64},{64,7... | collective-permute-start | bytes 307208 | tf_op jit(solution)/shard_map/ppermute | solution.py:15
  223.6 271.8 %reduce-scatter.11.cloned.1.call-start = ((), (), s32[]{:S(2)}) async-start(), calls=%async_computation.7 | async-start | bytes 1179648 | tf_op jit(solution)/shard_map/reduce_scatter | solution.py:147
  230.7 12.9 %collective-permute-start.7 = (f32[64,400]{1,0:T(8,128)S(1)}, f32[64,400]{1,0:T(8,128)S(1)}, u32[]{:S(2)}, u32[]{:S(2)}) collective-permute-start(f32[64,400]{1,0:T(8,128)S(1)} %broadcast_select_fusion.11), channel_id=1, source_target_pairs={{0,16},{8,24},{16,32},{24,40},{32,48},{40,56},{48,64},{56,72},{64,... | collective-permute-start | bytes 307208 | tf_op jit(solution)/shard_map/ppermute | solution.py:15
  243.6 17.5 %collective-permute-start.8 = (f32[64,400]{1,0:T(8,128)S(1)}, f32[64,400]{1,0:T(8,128)S(1)}, u32[]{:S(2)}, u32[]{:S(2)}) collective-permute-start(f32[64,400]{1,0:T(8,128)S(1)} %broadcast_select_fusion.13), channel_id=1, source_target_pairs={{0,32},{8,40},{16,48},{24,56},{32,64},{40,72},{48,80},{56,88},{64,... | collective-permute-start | bytes 307208 | tf_op jit(solution)/shard_map/ppermute | solution.py:15
  261.1 21.1 %collective-permute-start.9 = (f32[64,400]{1,0:T(8,128)S(1)}, f32[64,400]{1,0:T(8,128)S(1)}, u32[]{:S(2)}, u32[]{:S(2)}) collective-permute-start(f32[64,400]{1,0:T(8,128)S(1)} %broadcast_select_fusion.15), channel_id=1, source_target_pairs={{0,64},{8,72},{16,80},{24,88},{32,96},{40,104},{48,112},{56,120},{... | collective-permute-start | bytes 307208 | tf_op jit(solution)/shard_map/ppermute | solution.py:15
  282.2 8.2 %collective-permute-start.10 = (f32[64,400]{1,0:T(8,128)S(1)}, f32[64,400]{1,0:T(8,128)S(1)}, u32[]{:S(2)}, u32[]{:S(2)}) collective-permute-start(f32[64,400]{1,0:T(8,128)S(1)} %broadcast_select_fusion.17), channel_id=1, source_target_pairs={{0,128},{8,136},{16,144},{24,152},{32,160},{40,168},{48,176},{56,1... | collective-permute-start | bytes 307208 | tf_op jit(solution)/shard_map/ppermute | solution.py:15
  290.5 8.4 %collective-permute-start.11 = (f32[64,400]{1,0:T(8,128)S(1)}, f32[64,400]{1,0:T(8,128)S(1)}, u32[]{:S(2)}, u32[]{:S(2)}) collective-permute-start(f32[64,400]{1,0:T(8,128)S(1)} %broadcast_select_fusion.19), channel_id=1, source_target_pairs={{0,256},{8,264},{16,272},{24,280},{32,288},{40,296},{48,304},{56,3... | collective-permute-start | bytes 307208 | tf_op jit(solution)/shard_map/ppermute | solution.py:15
  299.9 0.7 copy-start.10
  300.5 6.1 %collective-permute-start.12 = (bf16[64,400]{1,0:T(8,128)(2,1)S(1)}, bf16[64,400]{1,0:T(8,128)(2,1)S(1)}, u32[]{:S(2)}, u32[]{:S(2)}) collective-permute-start(bf16[64,400]{1,0:T(8,128)(2,1)S(1)} %fusion.31), channel_id=1, source_target_pairs={{0,504},{8,0},{16,8},{24,16},{32,24},{40,32},{48,40},{56,48},{64,5... | collective-permute-start | bytes 153608 | tf_op jit(solution)/shard_map/ppermute | solution.py:15
  306.7 7.2 %collective-permute-start.13 = (bf16[64,400]{1,0:T(8,128)(2,1)S(1)}, bf16[64,400]{1,0:T(8,128)(2,1)S(1)}, u32[]{:S(2)}, u32[]{:S(2)}) collective-permute-start(bf16[64,400]{1,0:T(8,128)(2,1)S(1)} %broadcast_select_fusion.1), channel_id=1, source_target_pairs={{0,496},{8,504},{16,0},{24,8},{32,16},{40,24},{48,32},{56,40},{64,... | collective-permute-start | bytes 153608 | tf_op jit(solution)/shard_map/ppermute | solution.py:15
  313.9 11.3 %collective-permute-start.14 = (bf16[64,400]{1,0:T(8,128)(2,1)S(1)}, bf16[64,400]{1,0:T(8,128)(2,1)S(1)}, u32[]{:S(2)}, u32[]{:S(2)}) collective-permute-start(bf16[64,400]{1,0:T(8,128)(2,1)S(1)} %broadcast_select_fusion.3), channel_id=1, source_target_pairs={{0,480},{8,488},{16,496},{24,504},{32,0},{40,8},{48,16},{56,24},{6... | collective-permute-start | bytes 153608 | tf_op jit(solution)/shard_map/ppermute | solution.py:15
  325.2 14.9 %collective-permute-start.15 = (bf16[64,400]{1,0:T(8,128)(2,1)S(1)}, bf16[64,400]{1,0:T(8,128)(2,1)S(1)}, u32[]{:S(2)}, u32[]{:S(2)}) collective-permute-start(bf16[64,400]{1,0:T(8,128)(2,1)S(1)} %broadcast_select_fusion.5), channel_id=1, source_target_pairs={{0,448},{8,456},{16,464},{24,472},{32,480},{40,488},{48,496},{56,5... | collective-permute-start | bytes 153608 | tf_op jit(solution)/shard_map/ppermute | solution.py:15
  340.1 6.7 %collective-permute-start.16 = (bf16[64,400]{1,0:T(8,128)(2,1)S(1)}, bf16[64,400]{1,0:T(8,128)(2,1)S(1)}, u32[]{:S(2)}, u32[]{:S(2)}) collective-permute-start(bf16[64,400]{1,0:T(8,128)(2,1)S(1)} %broadcast_select_fusion.7), channel_id=1, source_target_pairs={{0,384},{8,392},{16,400},{24,408},{32,416},{40,424},{48,432},{56,4... | collective-permute-start | bytes 153608 | tf_op jit(solution)/shard_map/ppermute | solution.py:15
  346.9 16.5 %collective-permute-start.17 = (bf16[64,400]{1,0:T(8,128)(2,1)S(1)}, bf16[64,400]{1,0:T(8,128)(2,1)S(1)}, u32[]{:S(2)}, u32[]{:S(2)}) collective-permute-start(bf16[64,400]{1,0:T(8,128)(2,1)S(1)} %broadcast_select_fusion.9), channel_id=1, source_target_pairs={{0,256},{8,264},{16,272},{24,280},{32,288},{40,296},{48,304},{56,3... | collective-permute-start | bytes 153608 | tf_op jit(solution)/shard_map/ppermute | solution.py:15
  390.6 4.1 copy-start
  390.6 5.1 copy-start.6
  395.7 3.5 copy-start.1
  409.1 4.1 copy-start
  409.1 5.1 copy-start.6
  414.2 3.5 copy-start.1
  427.5 4.1 copy-start
  427.6 5.1 copy-start.6
  432.7 3.5 copy-start.1
  446.0 4.1 copy-start
  446.0 5.1 copy-start.6
  451.2 3.5 copy-start.1
  459.0 1.0 copy-start.5
  459.0 118.7 %copy-start.15 = (f32[64]{0:T(128)S(1)}, f32[64]{0:T(128)}, u32[]{:S(2)}) copy-start(f32[64]{0:T(128)} %param.14) | copy-start | bytes 772
  459.0 119.2 %copy-start.9 = (f32[64,400]{1,0:T(8,128)S(1)}, f32[64,400]{1,0:T(8,128)}, u32[]{:S(2)}) copy-start(f32[64,400]{1,0:T(8,128)} %param.13) | copy-start | bytes 307204
  459.0 119.2 %copy-start.11 = (f32[64,400]{1,0:T(8,128)S(1)}, f32[64,400]{1,0:T(8,128)}, u32[]{:S(2)}) copy-start(f32[64,400]{1,0:T(8,128)} %copy-done.10) | copy-start | bytes 307204
  460.0 110.8 %reduce-scatter.9.cloned.1.call-start = ((), (), s32[]{:S(2)}) async-start(), calls=%async_computation.6 | async-start | bytes 1179648 | tf_op jit(solution)/shard_map/reduce_scatter | solution.py:146
  495.3 12.0 %collective-permute-start.18 = (f32[64,400]{1,0:T(8,128)}, f32[64,400]{1,0:T(8,128)S(1)}, u32[]{:S(2)}, u32[]{:S(2)}) collective-permute-start(f32[64,400]{1,0:T(8,128)} %reduce-scatter.11.cloned.1.call-done), channel_id=1, source_target_pairs={{0,8},{8,16},{16,24},{24,32},{32,40},{40,48},{48,56},{56,64},{64,7... | collective-permute-start | bytes 307208 | tf_op jit(solution)/shard_map/ppermute | solution.py:15
  508.3 12.9 %collective-permute-start.19 = (f32[64,400]{1,0:T(8,128)S(1)}, f32[64,400]{1,0:T(8,128)S(1)}, u32[]{:S(2)}, u32[]{:S(2)}) collective-permute-start(f32[64,400]{1,0:T(8,128)S(1)} %broadcast_select_fusion), channel_id=1, source_target_pairs={{0,16},{8,24},{16,32},{24,40},{32,48},{40,56},{48,64},{56,72},{64,... | collective-permute-start | bytes 307208 | tf_op jit(solution)/shard_map/ppermute | solution.py:15
  521.3 17.5 %collective-permute-start.20 = (f32[64,400]{1,0:T(8,128)S(1)}, f32[64,400]{1,0:T(8,128)S(1)}, u32[]{:S(2)}, u32[]{:S(2)}) collective-permute-start(f32[64,400]{1,0:T(8,128)S(1)} %broadcast_select_fusion.2), channel_id=1, source_target_pairs={{0,32},{8,40},{16,48},{24,56},{32,64},{40,72},{48,80},{56,88},{64,... | collective-permute-start | bytes 307208 | tf_op jit(solution)/shard_map/ppermute | solution.py:15
  538.8 21.2 %collective-permute-start.21 = (f32[64,400]{1,0:T(8,128)S(1)}, f32[64,400]{1,0:T(8,128)S(1)}, u32[]{:S(2)}, u32[]{:S(2)}) collective-permute-start(f32[64,400]{1,0:T(8,128)S(1)} %broadcast_select_fusion.4), channel_id=1, source_target_pairs={{0,64},{8,72},{16,80},{24,88},{32,96},{40,104},{48,112},{56,120},{... | collective-permute-start | bytes 307208 | tf_op jit(solution)/shard_map/ppermute | solution.py:15
  560.0 8.3 %collective-permute-start.22 = (f32[64,400]{1,0:T(8,128)S(1)}, f32[64,400]{1,0:T(8,128)S(1)}, u32[]{:S(2)}, u32[]{:S(2)}) collective-permute-start(f32[64,400]{1,0:T(8,128)S(1)} %broadcast_select_fusion.6), channel_id=1, source_target_pairs={{0,128},{8,136},{16,144},{24,152},{32,160},{40,168},{48,176},{56,1... | collective-permute-start | bytes 307208 | tf_op jit(solution)/shard_map/ppermute | solution.py:15
  568.3 8.4 %collective-permute-start.23 = (f32[64,400]{1,0:T(8,128)S(1)}, f32[64,400]{1,0:T(8,128)S(1)}, u32[]{:S(2)}, u32[]{:S(2)}) collective-permute-start(f32[64,400]{1,0:T(8,128)S(1)} %broadcast_select_fusion.8), channel_id=1, source_target_pairs={{0,256},{8,264},{16,272},{24,280},{32,288},{40,296},{48,304},{56,3... | collective-permute-start | bytes 307208 | tf_op jit(solution)/shard_map/ppermute | solution.py:15
Sparse Core Ops, SparseCore 0:
  180.2 37.3 reduce-scatter.6
  223.7 37.7 reduce-scatter.4
  460.1 35.1 reduce-scatter.10
  501.3 37.7 reduce-scatter.8
where the time goes:
time: 588 us; the launch traced here: 586 us
  waiting for transfers between devices  214 us (36%)
  local copies, waits for them, and re-layouts  106 us (18%)
  starting transfers between devices  103 us (18%)
  matrix products  59.8 us (10%)
  blocking collectives  52.4 us (9%)
  other arithmetic  28 us (5%)
  between operations  21.1 us (4%)
    ppermute x24, waiting for transfers between devices, passed_along(): lax.ppermute(value, axis, [(i, (i + by) % count) for i in range(count)])  141 us
    ppermute x24, starting transfers between devices, passed_along(): lax.ppermute(value, axis, [(i, (i + by) % count) for i in range(count)])  103 us
    reduce_scatter x2, waiting for transfers between devices, body(): lax.psum_scatter(tail_part, 'row', scatter_dimension=0, tiled=True)  72.8 us
    gather x16, local copies, waits for them, and re-layouts, block_grads(): rel_rows = relation[rel_list].astype(jnp.float32)  39.2 us
    dot_general x16, matrix products, add_by_rows(): jnp.dot(selector, values, precision=lax.Precision.HIGHEST, preferred_elem...  32 us
    all_gather x2, blocking collectives, body(): lax.all_gather(working, 'row', axis=0, tiled=True)  26.2 us
    all_gather x2, blocking collectives, body(): lax.all_gather(far_shard, 'row', axis=0, tiled=True)  26.2 us
    gather x16, local copies, waits for them, and re-layouts, block_grads(): tails = tail_panel[tail_ids].astype(jnp.float32)  17.2 us
  transfers between devices with their start and end apart: 28, of which 22 were waited for; matrix products, arithmetic and copies ran while one was open for 3% of the time, Pallas kernels for 0%

commit v1 on v0

v1 whole, which is shorter than its diff:
```python
import jax
import jax.numpy as jnp
from jax import lax
from jax.experimental import pallas as pl
from jax.experimental.pallas import tpu as pltpu
from jax.sharding import PartitionSpec as P

ROUNDS = 2
D = 400
HALF = 200
WIDE = 512
PART = 4
LANES = 128
SUM_PIECE, SUM_LANE = 1, 127
ND, NR, NX = 64, 8, 4
R_DEV = 64
ROWS = 512
EDGES = 2048
NREL = 4096
NEG = 128
BLOCK = 256
BLOCKS = EDGES // BLOCK
LEARN = 0.1
MESH = pl.DeviceIdType.MESH
F32, BF16 = jnp.float32, jnp.bfloat16
NT = (((1,), (1,)), ((), ()))
TN = (((0,), (0,)), ((), ()))


def dot(a, b):
    return jnp.dot(a, b, preferred_element_type=F32)


def remote(src, dst, send, recv, device):
    return pltpu.make_async_remote_copy(
        src_ref=src, dst_ref=dst, send_sem=send, recv_sem=recv, device_id=device, device_id_type=MESH
    )


def panel_order(ids):
    owner = ids // R_DEV
    return (owner % 2) * (ROWS // 2) + (owner // 2) * R_DEV + ids % R_DEV


def as_column(row):
    return jnp.transpose(jnp.broadcast_to(row, (LANES, row.shape[1])))


def one_hot_rows(row, count):
    column = as_column(row)
    lane = lax.broadcasted_iota(jnp.int32, column.shape, 1)
    pieces = [(column == lane + first).astype(F32).astype(BF16) for first in range(0, count, LANES)]
    return jnp.concatenate(pieces, axis=1)


def one_hot_columns(row, count):
    place = lax.broadcasted_iota(jnp.int32, (count, row.shape[1]), 0)
    return (row == place).astype(F32).astype(BF16)


def split(value):
    high = value.astype(BF16)
    return high, (value - high.astype(F32)).astype(BF16)


def kernel(
    offsets, counts, state0, head0, lhs, rhs, rel, neg, relation,
    out,
    raw, table, rel_rows, hot_h, hot_t, hot_ht, hot_tt, query, grad_h, grad_t, neg_sum, neg_rows,
    state, work, stage, tail_in, head_in, shard_h, shard_t, panel_h, panel_t,
    acc_h, acc_t, near_h, near_t, far_send, far_h, far_t, row_send, got_h, got_t,
    raw_sem, a2a_send, a2a_recv, ag_send, ag_recv, rs_send, rs_recv,
):
    me, row = lax.axis_index("dom"), lax.axis_index("row")
    x, core = row // 2, lax.rem(row, 2)
    sibling = x * 2 + 1 - core
    slot = core * NX + x

    barrier = pltpu.get_barrier_semaphore()

    def greet(j, c):
        pl.semaphore_signal(barrier, inc=1, device_id=(lax.rem(me + j, ND), row), device_id_type=MESH)
        return c

    lax.fori_loop(1, ND, greet, 0)
    for j in range(1, NR):
        pl.semaphore_signal(barrier, inc=1, device_id=(me, lax.rem(row + j, NR)), device_id_type=MESH)

    def relation_block(k, b):
        at = pl.ds(pl.multiple_of(b * BLOCK, BLOCK), BLOCK)
        hot = one_hot_rows(rel[pl.ds(k, 1), at], NREL)
        rel_rows[k, at, :] = dot(hot, table[...]).astype(BF16)

    def relation_blocks(k, first, last):
        def step(b, c):
            relation_block(k, b)
            return c

        lax.fori_loop(first, last, step, 0)

    def selectors(k):
        def step(b, c):
            at = pl.ds(pl.multiple_of(b * BLOCK, BLOCK), BLOCK)
            head_ids = panel_order(lhs[pl.ds(k, 1), at])
            tail_ids = panel_order(rhs[pl.ds(k, 1), at])
            hot_h[at, :] = one_hot_rows(head_ids, ROWS)
            hot_t[at, :] = one_hot_rows(tail_ids, ROWS)
            hot_ht[:, at] = one_hot_columns(head_ids, ROWS)
            hot_tt[:, at] = one_hot_columns(tail_ids, ROWS)
            return c

        lax.fori_loop(0, BLOCKS, step, 0)

    def queries(k):
        panel = panel_h[k].reshape(ROWS, WIDE)

        def step(b, c):
            at = pl.ds(pl.multiple_of(b * BLOCK, BLOCK), BLOCK)
            heads = dot(hot_h[at, :], panel)
            rels = rel_rows[k, at, :].astype(F32)
            h_re, h_im = heads[:, :256], heads[:, 256:]
            c_re, c_im = rels[:, :256], rels[:, 256:]
            query[at, :256] = (h_re * c_re - h_im * c_im).astype(BF16)
            query[at, 256:] = (h_re * c_im + h_im * c_re).astype(BF16)
            return c

        lax.fori_loop(0, BLOCKS, step, 0)

    def edge_grads(k):
        panel = panel_t[k].reshape(ROWS, WIDE)
        neg_ids = panel_order(neg[pl.ds(k, 1), :])
        neg_rows[...] = dot(one_hot_rows(neg_ids, ROWS), panel).astype(BF16)
        neg_sum[...] = jnp.zeros_like(neg_sum)
        count = counts[k, 0]

        def step(b, c):
            at = pl.ds(pl.multiple_of(b * BLOCK, BLOCK), BLOCK)
            tails = dot(hot_t[at, :], panel)
            q = query[at, :]
            q_f = q.astype(F32)
            positive = jnp.sum(q_f * tails, axis=1, keepdims=True)
            negative = lax.dot_general(q, neg_rows[...], NT, preferred_element_type=F32)
            live = b * BLOCK + lax.broadcasted_iota(jnp.int32, (BLOCK, 1), 0) < count
            pos_weight = jnp.where(live, -1.0 / (1.0 + jnp.exp(positive)), 0.0)
            neg_weight = jnp.where(live, (1.0 / NEG) / (1.0 + jnp.exp(-negative)), 0.0).astype(BF16)
            g = pos_weight * tails + dot(neg_weight, neg_rows[...])
            rels = rel_rows[k, at, :].astype(F32)
            g_re, g_im = g[:, :256], g[:, 256:]
            c_re, c_im = rels[:, :256], rels[:, 256:]
            high, low = split(g_re * c_re + g_im * c_im)
            grad_h[0, at, :256] = high
            grad_h[1, at, :256] = low
            high, low = split(g_im * c_re - g_re * c_im)
            grad_h[0, at, 256:] = high
            grad_h[1, at, 256:] = low
            high, low = split(pos_weight * q_f)
            grad_t[0, at, :] = high
            grad_t[1, at, :] = low
            neg_sum[...] += lax.dot_general(neg_weight, q, TN, preferred_element_type=F32)
            return c

        lax.fori_loop(0, BLOCKS, step, 0)

    def tail_sums(k):
        hot_n = one_hot_columns(panel_order(neg[pl.ds(k, 1), :]), ROWS)
        high, low = split(neg_sum[...])
        total = dot(hot_tt[...], grad_t[0]) + dot(hot_tt[...], grad_t[1]) + dot(hot_n, high) + dot(hot_n, low)
        acc_t[k] = total.reshape(acc_t.shape[1:])

    def head_sums(k):
        total = dot(hot_ht[...], grad_h[0]) + dot(hot_ht[...], grad_h[1])
        acc_h[k] = total.reshape(acc_h.shape[1:])

    def spread(number, src, dst):
        def step(j, c):
            t = lax.rem(me + j, ND)
            remote(src.at[t], dst.at[me], a2a_send.at[number], a2a_recv.at[number], (t, row)).start()
            return c

        lax.fori_loop(1, ND, step, 0)
        dst[me] = src[me]

    def spread_wait(number, src, dst):
        most = pl.ds(0, ND - 1)
        remote(src.at[most], dst.at[most], a2a_send.at[number], a2a_recv.at[number], (lax.rem(me + 1, ND), row)).wait()

    def rotated(k, src, dst, forward):
        by = offsets[k]
        shift = by if forward else ND - by

        def step(j, c):
            dst[j] = src[lax.rem(j + shift, ND)]
            return c

        lax.fori_loop(0, ND, step, 0)

    def gather_copies(number, src, panel):
        out_copies = []
        for j in (2, 1, 3):
            t = lax.rem(x + j, NX) * 2 + core
            out_copies.append(
                remote(src, panel.at[slot], ag_send.at[number, j], ag_recv.at[number, j], (me, t))
            )
        own = remote(src, panel.at[slot], ag_send.at[number, 0], ag_recv.at[number, 0], (me, sibling))
        return out_copies, own

    def gather_start(number, src, panel):
        out_copies, own = gather_copies(number, src, panel)
        for copy in out_copies:
            copy.start()
        own.start()
        panel[slot] = src[...]

    def gather_finish(number, src, panel):
        out_copies, own = gather_copies(number, src, panel)
        passed = []
        for j, copy in ((1, out_copies[1]), (3, out_copies[2]), (2, out_copies[0])):
            copy.wait_recv()
            place = core * NX + lax.rem(x + NX - j, NX)
            onward = remote(
                panel.at[place], panel.at[place], ag_send.at[number, NX + j], ag_recv.at[number, NX + j], (me, sibling)
            )
            onward.start()
            passed.append(onward)
        for copy in out_copies:
            copy.wait_send()
        own.wait()
        for copy in passed:
            copy.wait()

    def near_copy(number, acc, near):
        other = pl.ds((1 - core) * NX, NX)
        return remote(acc.at[other], near, rs_send.at[number, 0], rs_recv.at[number, 0], (me, sibling))

    def far_copies(number, far):
        copies = []
        for j in (2, 1, 3):
            t = lax.rem(x + j, NX)
            copies.append(
                remote(
                    far_send.at[number, t], far.at[j], rs_send.at[number, j], rs_recv.at[number, j], (me, t * 2 + core)
                )
            )
        return copies

    def sum_near(number, acc, near, far):
        near_copy(number, acc, near).wait()
        near[...] = near[...] + acc[pl.ds(core * NX, NX)]
        far_send[number] = near[...].astype(BF16)
        for copy in far_copies(number, far):
            copy.start()

    def sum_far(number, near, far):
        for copy in far_copies(number, far):
            copy.wait()
        return near[x] + (far[1].astype(F32) + far[2].astype(F32) + far[3].astype(F32))

    def is_sum():
        piece = lax.broadcasted_iota(jnp.int32, state.shape, 1)
        lane = lax.broadcasted_iota(jnp.int32, state.shape, 2)
        return (piece == SUM_PIECE) & (lane == SUM_LANE)

    def to_work():
        work[...] = jnp.where(is_sum(), 0.0, state[...]).astype(BF16)

    def update(k):
        rotated(k, got_t.at[k], stage.at[2 + k], False)
        gradient = got_h[k].astype(F32) + stage[2 + k].astype(F32)
        at_sum = is_sum()
        now = state[...]
        squares = jnp.sum(jnp.where(at_sum, now, 0.0), axis=(1, 2), keepdims=True)
        squares = squares + jnp.sum(gradient * gradient, axis=(1, 2), keepdims=True) / D
        state[...] = jnp.where(at_sum, squares, now - LEARN * gradient / jnp.sqrt(squares))

    def to_rows(value):
        return value.reshape(R_DEV, PART, LANES).astype(BF16)

    def to_shard(value):
        return value.astype(F32).reshape(R_DEV, WIDE).astype(BF16)

    fetch = pltpu.make_async_copy(relation, raw, raw_sem.at[0])
    fetch.start()
    selectors(0)
    fetch.wait()
    from_col = lax.broadcasted_iota(jnp.int32, (D, WIDE), 0)
    to_col = lax.broadcasted_iota(jnp.int32, (D, WIDE), 1)
    widen = (to_col == jnp.where(from_col < HALF, from_col, from_col + 56)).astype(F32).astype(BF16)

    def widen_step(b, c):
        at = pl.ds(pl.multiple_of(b * BLOCK, BLOCK), BLOCK)
        table[at, :] = dot(raw[at, :], widen).astype(BF16)
        return c

    lax.fori_loop(0, NREL // BLOCK, widen_step, 0)
    relation_blocks(0, 0, 2)

    pl.semaphore_wait(barrier, ND - 1 + NR - 1)
    spread(0, state0, state)
    gather_start(0, head0, panel_h.at[0])
    relation_blocks(0, 2, 6)
    gather_finish(0, head0, panel_h.at[0])
    spread_wait(0, state0, state)
    to_work()
    rotated(0, work, stage.at[0], True)
    spread(1, stage.at[0], tail_in.at[0])
    relation_blocks(0, 6, 8)
    queries(0)
    spread_wait(1, stage.at[0], tail_in.at[0])
    shard_t[0] = to_shard(tail_in[0])
    gather_start(1, shard_t.at[0], panel_t.at[0])
    relation_blocks(1, 0, 3)
    gather_finish(1, shard_t.at[0], panel_t.at[0])

    for k in range(ROUNDS):
        if k > 0:
            spread_wait(4, work, head_in)
            shard_h[...] = to_shard(head_in[...])
            gather_start(2, shard_h, panel_h.at[1])
            spread_wait(5, stage.at[1], tail_in.at[1])
            shard_t[1] = to_shard(tail_in[1])
            gather_start(3, shard_t.at[1], panel_t.at[1])
            gather_finish(2, shard_h, panel_h.at[1])
            queries(1)
            gather_finish(3, shard_t.at[1], panel_t.at[1])
        edge_grads(k)
        tail_sums(k)
        near_copy(2 * k, acc_t.at[k], near_t.at[k]).start()
        head_sums(k)
        near_copy(2 * k + 1, acc_h.at[k], near_h.at[k]).start()
        sum_near(2 * k, acc_t.at[k], near_t.at[k], far_t.at[k])
        sum_near(2 * k + 1, acc_h.at[k], near_h.at[k], far_h.at[k])
        if k == 0:
            relation_blocks(1, 3, 6)
        row_send[2 * k] = to_rows(sum_far(2 * k, near_t.at[k], far_t.at[k]))
        spread(2 + 4 * k, row_send.at[2 * k], got_t.at[k])
        row_send[2 * k + 1] = to_rows(sum_far(2 * k + 1, near_h.at[k], far_h.at[k]))
        spread(3 + 4 * k, row_send.at[2 * k + 1], got_h.at[k])
        if k == 0:
            relation_blocks(1, 6, 8)
            selectors(1)
        spread_wait(2 + 4 * k, row_send.at[2 * k], got_t.at[k])
        spread_wait(3 + 4 * k, row_send.at[2 * k + 1], got_h.at[k])
        update(k)
        if k == 0:
            to_work()
            spread(4, work, head_in)
            rotated(1, work, stage.at[1], True)
            spread(5, stage.at[1], tail_in.at[1])
    spread(8, state, out)
    spread_wait(8, state, out)


def body(embedding, adagrad, relation, offsets, counts, lhs_index, rhs_index, rel_ids, neg_index):
    gap = jnp.zeros((R_DEV, 256 - HALF), F32)
    wide = jnp.concatenate([embedding[:, :HALF], gap, embedding[:, HALF:], gap], axis=1)
    with_sum = jnp.concatenate(
        [embedding[:, :HALF], gap[:, 1:], adagrad[:, None], embedding[:, HALF:], gap], axis=1
    )
    vmem = pl.BlockSpec(memory_space=pltpu.VMEM)
    smem = pl.BlockSpec(memory_space=pltpu.SMEM)
    rows = (R_DEV, PART, LANES)
    panel = (NR, R_DEV, WIDE)
    half = (NX, R_DEV, WIDE)
    V = pltpu.VMEM
    result = pl.pallas_call(
        kernel,
        out_shape=jax.ShapeDtypeStruct(rows, F32),
        in_specs=[smem, smem] + [vmem] * 6 + [pl.BlockSpec(memory_space=pl.ANY)],
        out_specs=vmem,
        scratch_shapes=[
            V((NREL, D), BF16),
            V((NREL, WIDE), BF16),
            V((ROUNDS, EDGES, WIDE), BF16),
            V((EDGES, ROWS), BF16),
            V((EDGES, ROWS), BF16),
            V((ROWS, EDGES), BF16),
            V((ROWS, EDGES), BF16),
            V((EDGES, WIDE), BF16),
            V((2, EDGES, WIDE), BF16),
            V((2, EDGES, WIDE), BF16),
            V((NEG, WIDE), F32),
            V((NEG, WIDE), BF16),
            V(rows, F32),
            V(rows, BF16),
            V((4,) + rows, BF16),
            V((ROUNDS,) + rows, BF16),
            V(rows, BF16),
            V((R_DEV, WIDE), BF16),
            V((ROUNDS, R_DEV, WIDE), BF16),
            V((ROUNDS,) + panel, BF16),
            V((ROUNDS,) + panel, BF16),
            V((ROUNDS,) + panel, F32),
            V((ROUNDS,) + panel, F32),
            V((ROUNDS,) + half, F32),
            V((ROUNDS,) + half, F32),
            V((2 * ROUNDS,) + half, BF16),
            V((ROUNDS,) + half, BF16),
            V((ROUNDS,) + half, BF16),
            V((2 * ROUNDS,) + rows, BF16),
            V((ROUNDS,) + rows, BF16),
            V((ROUNDS,) + rows, BF16),
            pltpu.SemaphoreType.DMA((1,)),
            pltpu.SemaphoreType.DMA((9,)),
            pltpu.SemaphoreType.DMA((9,)),
            pltpu.SemaphoreType.DMA((4, 8)),
            pltpu.SemaphoreType.DMA((4, 8)),
            pltpu.SemaphoreType.DMA((4, 4)),
            pltpu.SemaphoreType.DMA((4, 4)),
        ],
        compiler_params=pltpu.CompilerParams(
            collective_id=0, has_side_effects=True, vmem_limit_bytes=60 * 1024 * 1024
        ),
        name="train",
    )(
        offsets,
        counts,
        with_sum.reshape(rows),
        wide.astype(BF16),
        lhs_index,
        rhs_index,
        rel_ids,
        neg_index.reshape(ROUNDS, NEG),
        relation,
    ).reshape(R_DEV, WIDE)
    embedding_out = jnp.concatenate([result[:, :HALF], result[:, 256 : 256 + HALF]], axis=1)
    return (embedding_out, result[:, 255])


def solution(mesh):
    return jax.shard_map(
        body,
        mesh=mesh,
        in_specs=(
            P(("dom", "row"), None),
            P(("dom", "row")),
            P(),
            P(),
            P(None, ("dom", "row")),
            P(None, ("dom", "row")),
            P(None, ("dom", "row")),
            P(None, ("dom", "row")),
            P(None, "dom", None),
        ),
        out_specs=(P(("dom", "row"), None), P(("dom", "row"))),
        check_vma=False,
    )
```

time: 588 us -> 157 us (0.27)
  waiting for transfers between devices: 214 us -> 0 us
  Pallas kernels: 0 us -> 141 us
  starting transfers between devices: 103 us -> 0 us
  local copies, waits for them, and re-layouts: 106 us -> 12.6 us
  matrix products: 59.8 us -> 0 us
  blocking collectives: 52.4 us -> 0 us
  other arithmetic: 28 us -> 1.46 us
  between operations: 21.1 us -> 0.67 us
    pallas_call x0 -> x1, Pallas kernels: none -> 141 us  [body(): pl.pallas_call(kernel, out_shape=jax.ShapeDtypeStruct(rows, F32), in_spec...]
    ppermute x24 -> x0, waiting for transfers between devices: 141 us -> none  [passed_along(): lax.ppermute(value, axis, [(i, (i + by) % count) for i in range(count)])]
    ppermute x24 -> x0, starting transfers between devices: 103 us -> none  [passed_along(): lax.ppermute(value, axis, [(i, (i + by) % count) for i in range(count)])]
    gather x50 -> x0, local copies, waits for them, and re-layouts: 76.6 us -> none  [the longest x16 39.2 us: block_grads(): rel_rows = relation[rel_list].astype(jnp.float32)]
    reduce_scatter x4 -> x0, waiting for transfers between devices: 72.8 us -> none  [the longest x2 72.8 us: body(): lax.psum_scatter(tail_part, 'row', scatter_dimension=0, tiled=True)]
    dot_general x40 -> x0, matrix products: 59.8 us -> none  [the longest x16 32 us: add_by_rows(): jnp.dot(selector, values, precision=lax.Precision.HIGHEST, preferred_elem...]
    all_gather x4 -> x0, blocking collectives: 52.4 us -> none  [the longest x2 26.2 us: body(): lax.all_gather(working, 'row', axis=0, tiled=True)]
    while x55 -> x0, local copies, waits for them, and re-layouts: 16.1 us -> none  [the longest x7 16 us: device_grads(): lax.fori_loop(0, block_count, step, (zero_rows, zero_rows, zero_negs))]
  transfers between devices with their start and end apart: 28 -> 0, of which waited for: 22 -> 0; matrix products, arithmetic and copies ran while one was open for 3% -> 0% of each run, Pallas kernels for 0% -> 0%
where the time goes in v1:
time: 157 us; the launch traced here: 156 us
  Pallas kernels  141 us (90%)
  local copies, waits for them, and re-layouts  12.6 us (8%)
    pallas_call x1, Pallas kernels, body(): pl.pallas_call(kernel, out_shape=jax.ShapeDtypeStruct(rows, F32), in_spec...  141 us
    unnamed x3, local copies, waits for them, and re-layouts  8.26 us

profile of v1, /device:TPU:6, one launch (start us, length us, event | category | flops | bytes accessed | tf_op | source)
XLA Modules:
  0.0 156.2 jit_solution(15282116459809002697)
XLA Ops:
  0.6 1.3 copy.15.counts
  2.0 0.7 copy.14
  2.7 1.1 fusion.1
  3.8 0.7 pad_maximum_fusion.1.head0
  4.5 1.0 fusion.2
  5.5 0.1 concatenate.10
  5.6 0.7 reshape.13.state0
  6.3 6.0 %copy.16.relation = bf16[4096,400]{1,0:T(8,128)(2,1)} copy(bf16[4096,400]{0,1:T(8,128)(2,1)} %param.11) | data formatting | bytes 6553600 | tf_op args[2]
  12.3 141.5 %train.1 = f32[64,4,128]{2,1,0:T(4,128)} custom-call(s32[2]{0:T(128)} %offsets.1, s32[2,1]{1,0:T(2,128)} %copy.15.counts, f32[64,4,128]{2,1,0:T(4,128)} %reshape.13.state0, bf16[64,512]{1,0:T(8,128)(2,1)} %pad_maximum_fusion.1.head0, s32[2,2048]{1,0:T(2,128)} %lhs.2, s32[2,2048]{1,0:T(2,128)} %rhs.2, s32[2,2048]{1,0:T(2,128)} %rel.1, s32[2,128]{1,0:T(2,128)} %bitcast.9, ...), custom_call_target="tpu_custom_call" | custom-call | tf_op jit(solution)/shard_map/train/pallas_call | solution.py:365
  153.8 0.9 copy.19
  154.7 0.7 slice_reduce_fusion
  155.4 0.8 pad_maximum_fusion
  (4 shorter events, 0.0 us)

commit v2 on v1

v2 whole, which is shorter than its diff:
```python
import jax
import jax.numpy as jnp
from jax import lax
from jax.experimental import pallas as pl
from jax.experimental.pallas import tpu as pltpu
from jax.sharding import PartitionSpec as P

ROUNDS = 2
D = 400
HALF = 200
WIDE = 512
PART = 4
LANES = 128
SUM_PIECE, SUM_LANE = 1, 127
ND, NR, NX, NY, NZ = 64, 8, 4, 4, 16
R_DEV = 64
ROWS = 512
EDGES = 2048
NREL = 4096
NEG = 128
BLOCK = 256
BLOCKS = EDGES // BLOCK
STEP = 2048
STEPS = EDGES // STEP
LEARN = 0.1
MESH = pl.DeviceIdType.MESH
F32, BF16 = jnp.float32, jnp.bfloat16
NT = (((1,), (1,)), ((), ()))
TN = (((0,), (0,)), ((), ()))


def dot(a, b):
    return jnp.dot(a, b, preferred_element_type=F32)


def remote(src, dst, send, recv, device):
    return pltpu.make_async_remote_copy(
        src_ref=src, dst_ref=dst, send_sem=send, recv_sem=recv, device_id=device, device_id_type=MESH
    )


def panel_order(ids):
    owner = ids // R_DEV
    return (owner % 2) * (ROWS // 2) + (owner // 2) * R_DEV + ids % R_DEV


def as_column(row):
    return jnp.transpose(jnp.broadcast_to(row, (LANES, row.shape[1])))


def one_hot_rows(row, count):
    column = as_column(row)
    lane = lax.broadcasted_iota(jnp.int32, column.shape, 1)
    pieces = [(column == lane + first).astype(F32).astype(BF16) for first in range(0, count, LANES)]
    return jnp.concatenate(pieces, axis=1)


def one_hot_columns(row, count):
    place = lax.broadcasted_iota(jnp.int32, (count, row.shape[1]), 0)
    return (row == place).astype(F32).astype(BF16)


def split(value):
    high = value.astype(BF16)
    return high, (value - high.astype(F32)).astype(BF16)


def kernel(
    offsets, counts, embedding, adagrad, lhs, rhs, rel, neg, relation,
    out,
    raw, work0, state0, head0, home, home_t, rel_rows, hot_h, hot_t, hot_ht, hot_tt, query, tail_rows, pos_weights, neg_weights, grad_h, grad_t, neg_sum, neg_rows,
    state, work, stage, tail_in, head_in, shard_h, shard_t, panel_h, panel_t,
    acc_h, acc_t, near_h, near_t, far_send, far_h, far_t, row_send, got_h, got_t,
    raw_sem, a2a_send, a2a_recv, ag_send, ag_recv, rs_send, rs_recv,
):
    me, row = lax.axis_index("dom"), lax.axis_index("row")
    x, core = row // 2, lax.rem(row, 2)
    y, z = me // NZ, lax.rem(me, NZ)
    sibling = x * 2 + 1 - core
    slot = core * NX + x

    barrier = pltpu.get_barrier_semaphore()

    def greet(j, c):
        pl.semaphore_signal(barrier, inc=1, device_id=(lax.rem(me + j, ND), row), device_id_type=MESH)
        return c

    lax.fori_loop(1, ND, greet, 0)
    for j in range(1, NR):
        pl.semaphore_signal(barrier, inc=1, device_id=(me, lax.rem(row + j, NR)), device_id_type=MESH)

    gap = jnp.zeros((R_DEV, 256 - HALF), F32)
    wide = jnp.concatenate([embedding[:, :HALF], gap, embedding[:, HALF:], gap], axis=1)
    column = lax.broadcasted_iota(jnp.int32, (R_DEV, WIDE), 1)
    sums = as_column(jnp.concatenate([adagrad[...], adagrad[...]], axis=1))[:R_DEV, :1]
    state0[...] = jnp.where(column == SUM_PIECE * LANES + SUM_LANE, sums, wide).reshape(state0.shape)
    head0[...] = wide.astype(BF16)
    work0[...] = wide.reshape(work0.shape).astype(BF16)

    def relation_block(k, b):
        at = pl.ds(pl.multiple_of(b * BLOCK, BLOCK), BLOCK)
        found = dot(raw[...], one_hot_columns(rel[pl.ds(k, 1), at], NREL))
        hole = jnp.zeros((256 - HALF, BLOCK), F32)
        spaced = jnp.concatenate([found[:HALF], hole, found[HALF:], hole], axis=0)
        rel_rows[k, at, :] = jnp.transpose(spaced).astype(BF16)

    def relation_blocks(k, first, last):
        def step(b, c):
            relation_block(k, b)
            return c

        lax.fori_loop(first, last, step, 0)

    def selectors(k):
        def step(b, c):
            at = pl.ds(pl.multiple_of(b * BLOCK, BLOCK), BLOCK)
            head_ids = panel_order(lhs[pl.ds(k, 1), at])
            tail_ids = panel_order(rhs[pl.ds(k, 1), at])
            hot_h[at, :] = one_hot_rows(head_ids, ROWS)
            hot_t[at, :] = one_hot_rows(tail_ids, ROWS)
            hot_ht[:, at] = one_hot_columns(head_ids, ROWS)
            hot_tt[:, at] = one_hot_columns(tail_ids, ROWS)
            return c

        lax.fori_loop(0, BLOCKS, step, 0)

    def queries(k):
        panel = panel_h[k].reshape(ROWS, WIDE)

        def step(b, c):
            at = pl.ds(pl.multiple_of(b * STEP, STEP), STEP)
            heads = dot(hot_h[at, :], panel)
            rels = rel_rows[k, at, :].astype(F32)
            h_re, h_im = heads[:, :256], heads[:, 256:]
            c_re, c_im = rels[:, :256], rels[:, 256:]
            query[at, :256] = (h_re * c_re - h_im * c_im).astype(BF16)
            query[at, 256:] = (h_re * c_im + h_im * c_re).astype(BF16)
            return c

        lax.fori_loop(0, STEPS, step, 0)

    def tail_grads(k):
        panel = panel_t[k].reshape(ROWS, WIDE)
        neg_ids = panel_order(neg[pl.ds(k, 1), :])
        negatives = dot(one_hot_rows(neg_ids, ROWS), panel)
        neg_rows[...] = negatives.astype(BF16)
        neg_turned = jnp.transpose(negatives).astype(BF16)
        neg_sum[...] = jnp.zeros_like(neg_sum)
        count = counts[k]

        def step(b, c):
            at = pl.ds(pl.multiple_of(b * STEP, STEP), STEP)
            tails = dot(hot_t[at, :], panel)
            tail_rows[at, :] = tails.astype(BF16)
            q = query[at, :]
            q_f = q.astype(F32)
            positive = jnp.sum(q_f * tails, axis=1, keepdims=True)
            negative = dot(q, neg_turned)
            live = b * STEP + lax.broadcasted_iota(jnp.int32, (STEP, 1), 0) < count
            pos_weight = jnp.where(live, -1.0 / (1.0 + jnp.exp(positive)), 0.0)
            neg_weight = jnp.where(live, (1.0 / NEG) / (1.0 + jnp.exp(-negative)), 0.0).astype(BF16)
            pos_weights[at, :] = pos_weight
            neg_weights[at, :] = neg_weight
            high, low = split(pos_weight * q_f)
            grad_t[0, at, :] = high
            grad_t[1, at, :] = low
            neg_sum[...] += lax.dot_general(neg_weight, q, TN, preferred_element_type=F32)
            return c

        lax.fori_loop(0, STEPS, step, 0)

    def head_grads(k):
        def step(b, c):
            at = pl.ds(pl.multiple_of(b * STEP, STEP), STEP)
            g = pos_weights[at, :] * tail_rows[at, :].astype(F32) + dot(neg_weights[at, :], neg_rows[...])
            rels = rel_rows[k, at, :].astype(F32)
            g_re, g_im = g[:, :256], g[:, 256:]
            c_re, c_im = rels[:, :256], rels[:, 256:]
            high, low = split(g_re * c_re + g_im * c_im)
            grad_h[0, at, :256] = high
            grad_h[1, at, :256] = low
            high, low = split(g_im * c_re - g_re * c_im)
            grad_h[0, at, 256:] = high
            grad_h[1, at, 256:] = low
            return c

        lax.fori_loop(0, STEPS, step, 0)

    def tail_sums(k, half):
        rows = pl.ds(half * (ROWS // 2), ROWS // 2)
        hot_n = one_hot_columns(panel_order(neg[pl.ds(k, 1), :]) - half * (ROWS // 2), ROWS // 2)
        high, low = split(neg_sum[...])
        total = dot(hot_tt[rows, :], grad_t[0]) + dot(hot_tt[rows, :], grad_t[1]) + dot(hot_n, high) + dot(hot_n, low)
        acc_t[k, pl.ds(half * NX, NX)] = total.reshape(NX, R_DEV, WIDE)

    def head_sums(k, half):
        rows = pl.ds(half * (ROWS // 2), ROWS // 2)
        total = dot(hot_ht[rows, :], grad_h[0]) + dot(hot_ht[rows, :], grad_h[1])
        acc_h[k, pl.ds(half * NX, NX)] = total.reshape(NX, R_DEV, WIDE)

    def spread(number, src, dst):
        def send(dy, dz):
            t = lax.rem(y + dy, NY) * NZ + lax.rem(z + dz, NZ)
            remote(src.at[t], dst.at[me], a2a_send.at[number], a2a_recv.at[number], (t, row)).start()

        def step(i, c):
            dz = NZ // 2 + (i + 1) // 2 * (1 - 2 * (i % 2))
            for dy in (2, 1, 3, 0):
                send(dy, dz)
            return c

        lax.fori_loop(0, NZ - 1, step, 0)
        for dy in (2, 1, 3):
            send(dy, 0)
        dst[me] = src[me]

    def spread_wait(number, src, dst):
        most = pl.ds(0, ND - 1)
        remote(src.at[most], dst.at[most], a2a_send.at[number], a2a_recv.at[number], (lax.rem(me + 1, ND), row)).wait()

    def rotated(k, src, dst, forward):
        by = offsets[k]
        shift = by if forward else ND - by

        def step(j, c):
            dst[j] = src[lax.rem(j + shift, ND)]
            return c

        lax.fori_loop(0, ND, step, 0)

    def gather_far(number, src, panel):
        copies = []
        for j in (2, 1, 3):
            t = lax.rem(x + j, NX) * 2 + core
            copies.append(remote(src, panel.at[slot], ag_send.at[number, j], ag_recv.at[number, j], (me, t)))
        return copies

    def gather_near(number, src, panel):
        return remote(src, panel.at[slot], ag_send.at[number, 0], ag_recv.at[number, 0], (me, sibling))

    def gather_start(number, src, panel):
        for copy in gather_far(number, src, panel):
            copy.start()
        gather_near(number, src, panel).start()
        panel[slot] = src[...]

    def gather_passed(number, panel):
        copies = []
        for j in (1, 3, 2):
            place = core * NX + lax.rem(x + NX - j, NX)
            copies.append(
                remote(
                    panel.at[place], panel.at[place], ag_send.at[number, NX + j], ag_recv.at[number, NX + j], (me, sibling)
                )
            )
        return copies

    def gather_pass(number, src, panel):
        opposite, right, left = gather_far(number, src, panel)
        for came, onward in zip((right, left, opposite), gather_passed(number, panel)):
            came.wait_recv()
            onward.start()

    def gather_end(number, src, panel):
        for copy in gather_far(number, src, panel):
            copy.wait_send()
        gather_near(number, src, panel).wait()
        for copy in gather_passed(number, panel):
            copy.wait()

    def near_copy(number, acc, near):
        other = pl.ds((1 - core) * NX, NX)
        return remote(acc.at[other], near, rs_send.at[number, 0], rs_recv.at[number, 0], (me, sibling))

    def far_copies(number, far):
        copies = []
        for j in (2, 1, 3):
            t = lax.rem(x + j, NX)
            copies.append(
                remote(
                    far_send.at[number, t], far.at[j], rs_send.at[number, j], rs_recv.at[number, j], (me, t * 2 + core)
                )
            )
        return copies

    def sum_near(number, acc, near, far):
        near_copy(number, acc, near).wait()
        near[...] = near[...] + acc[pl.ds(core * NX, NX)]
        far_send[number] = near[...].astype(BF16)
        for copy in far_copies(number, far):
            copy.start()

    def sum_far(number, near, far):
        for copy in far_copies(number, far):
            copy.wait()
        return near[x] + (far[1].astype(F32) + far[2].astype(F32) + far[3].astype(F32))

    def is_sum():
        piece = lax.broadcasted_iota(jnp.int32, state.shape, 1)
        lane = lax.broadcasted_iota(jnp.int32, state.shape, 2)
        return (piece == SUM_PIECE) & (lane == SUM_LANE)

    def update(k):
        rotated(k, got_t.at[k], stage.at[2 + k], False)
        gradient = got_h[...].astype(F32) + stage[2 + k].astype(F32)
        at_sum = is_sum()
        now = state[...]
        squares = jnp.sum(jnp.where(at_sum, now, 0.0), axis=(1, 2), keepdims=True)
        squares = squares + jnp.sum(gradient * gradient, axis=(1, 2), keepdims=True) / D
        state[...] = jnp.where(at_sum, squares, now - LEARN * gradient / jnp.sqrt(squares))

    def finish(head_sum):
        gradient = head_sum + home_t[...].astype(F32).reshape(R_DEV, WIDE)
        now = home[...].reshape(R_DEV, WIDE)
        place = SUM_PIECE * LANES + SUM_LANE
        squares = now[:, place : place + 1] + jnp.sum(gradient * gradient, axis=1, keepdims=True) / D
        now = now - LEARN * gradient / jnp.sqrt(squares)
        column = lax.broadcasted_iota(jnp.int32, now.shape, 1)
        out[...] = jnp.where(column == place, squares, now)

    def to_rows(value):
        return value.reshape(R_DEV, PART, LANES).astype(BF16)

    def to_shard(value):
        return value.astype(F32).reshape(R_DEV, WIDE).astype(BF16)

    fetch = pltpu.make_async_copy(relation, raw, raw_sem.at[0])
    fetch.start()
    selectors(0)
    fetch.wait()
    relation_blocks(0, 0, 2)

    pl.semaphore_wait(barrier, ND - 1 + NR - 1)
    spread(0, work0, work)
    gather_start(0, head0, panel_h.at[0])
    relation_blocks(0, 2, 5)
    gather_pass(0, head0, panel_h.at[0])
    relation_blocks(0, 5, 7)
    spread_wait(0, work0, work)
    rotated(0, work, stage.at[0], True)
    spread(1, stage.at[0], tail_in.at[0])
    relation_blocks(0, 7, 8)
    gather_end(0, head0, panel_h.at[0])
    queries(0)
    spread_wait(1, stage.at[0], tail_in.at[0])
    shard_t[0] = to_shard(tail_in[0])
    gather_start(1, shard_t.at[0], panel_t.at[0])
    spread(9, state0, state)
    relation_blocks(1, 0, 2)
    gather_pass(1, shard_t.at[0], panel_t.at[0])
    relation_blocks(1, 2, 3)
    gather_end(1, shard_t.at[0], panel_t.at[0])

    for k in range(ROUNDS):
        last = k == ROUNDS - 1
        if k > 0:
            spread_wait(4, work, head_in)
            shard_h[...] = to_shard(head_in[...])
            gather_start(2, shard_h, panel_h.at[1])
            spread_wait(5, stage.at[1], tail_in.at[1])
            shard_t[1] = to_shard(tail_in[1])
            gather_start(3, shard_t.at[1], panel_t.at[1])
            gather_pass(2, shard_h, panel_h.at[1])
            gather_end(2, shard_h, panel_h.at[1])
            gather_pass(3, shard_t.at[1], panel_t.at[1])
            queries(1)
            gather_end(3, shard_t.at[1], panel_t.at[1])
        tail_grads(k)
        tail_sums(k, 1 - core)
        near_copy(2 * k, acc_t.at[k], near_t.at[k]).start()
        tail_sums(k, core)
        head_grads(k)
        sum_near(2 * k, acc_t.at[k], near_t.at[k], far_t.at[k])
        head_sums(k, 1 - core)
        near_copy(2 * k + 1, acc_h.at[k], near_h.at[k]).start()
        head_sums(k, core)
        if not last:
            relation_blocks(1, 3, 4)
        sum_near(2 * k + 1, acc_h.at[k], near_h.at[k], far_h.at[k])
        row_send[2 * k] = to_rows(sum_far(2 * k, near_t.at[k], far_t.at[k]))
        spread(2 + 4 * k, row_send.at[2 * k], got_t.at[k])
        if not last:
            relation_blocks(1, 4, 6)
            row_send[1] = to_rows(sum_far(1, near_h.at[0], far_h.at[0]))
            spread(3, row_send.at[1], got_h)
            relation_blocks(1, 6, 8)
            selectors(1)
            spread_wait(9, state0, state)
            spread_wait(2, row_send.at[0], got_t.at[0])
            spread_wait(3, row_send.at[1], got_h)
            update(0)
            work[...] = jnp.where(is_sum(), 0.0, state[...]).astype(BF16)
            spread(4, work, head_in)
            rotated(1, work, stage.at[1], True)
            spread(5, stage.at[1], tail_in.at[1])
            spread(7, state, home)
        else:
            head_sum = sum_far(2 * k + 1, near_h.at[k], far_h.at[k])
            spread_wait(7, state, home)
            spread_wait(6, row_send.at[2], got_t.at[1])
            rotated(1, got_t.at[1], stage.at[3], False)
            spread(8, stage.at[3], home_t)
            spread_wait(8, stage.at[3], home_t)
            finish(head_sum)


def narrow(state, embedding_out, adagrad_out):
    now = state[...]
    embedding_out[...] = jnp.concatenate([now[:, :HALF], now[:, 256 : 256 + HALF]], axis=1)
    place = SUM_PIECE * LANES + SUM_LANE
    squares = jnp.broadcast_to(now[:, place : place + 1], (R_DEV, LANES))
    adagrad_out[...] = jnp.transpose(jnp.concatenate([squares, squares], axis=0))[:1, :R_DEV]


def body(embedding, adagrad, relation, offsets, counts, lhs_index, rhs_index, rel_ids, neg_index):
    vmem = pl.BlockSpec(memory_space=pltpu.VMEM)
    smem = pl.BlockSpec(memory_space=pltpu.SMEM)
    rows = (R_DEV, PART, LANES)
    panel = (NR, R_DEV, WIDE)
    half = (NX, R_DEV, WIDE)
    V = pltpu.VMEM
    state = pl.pallas_call(
        kernel,
        out_shape=jax.ShapeDtypeStruct((R_DEV, WIDE), F32),
        in_specs=[smem, smem] + [vmem] * 6 + [pl.BlockSpec(memory_space=pl.ANY)],
        out_specs=vmem,
        scratch_shapes=[
            V((D, NREL), BF16),
            V(rows, BF16),
            V(rows, F32),
            V((R_DEV, WIDE), BF16),
            V(rows, F32),
            V(rows, BF16),
            V((ROUNDS, EDGES, WIDE), BF16),
            V((EDGES, ROWS), BF16),
            V((EDGES, ROWS), BF16),
            V((ROWS, EDGES), BF16),
            V((ROWS, EDGES), BF16),
            V((EDGES, WIDE), BF16),
            V((EDGES, WIDE), BF16),
            V((EDGES, 1), F32),
            V((EDGES, NEG), BF16),
            V((2, EDGES, WIDE), BF16),
            V((2, EDGES, WIDE), BF16),
            V((NEG, WIDE), F32),
            V((NEG, WIDE), BF16),
            V(rows, F32),
            V(rows, BF16),
            V((4,) + rows, BF16),
            V((ROUNDS,) + rows, BF16),
            V(rows, BF16),
            V((R_DEV, WIDE), BF16),
            V((ROUNDS, R_DEV, WIDE), BF16),
            V((ROUNDS,) + panel, BF16),
            V((ROUNDS,) + panel, BF16),
            V((ROUNDS,) + panel, F32),
            V((ROUNDS,) + panel, F32),
            V((ROUNDS,) + half, F32),
            V((ROUNDS,) + half, F32),
            V((2 * ROUNDS,) + half, BF16),
            V((ROUNDS,) + half, BF16),
            V((ROUNDS,) + half, BF16),
            V((3,) + rows, BF16),
            V(rows, BF16),
            V((ROUNDS,) + rows, BF16),
            pltpu.SemaphoreType.DMA((1,)),
            pltpu.SemaphoreType.DMA((10,)),
            pltpu.SemaphoreType.DMA((10,)),
            pltpu.SemaphoreType.DMA((4, 8)),
            pltpu.SemaphoreType.DMA((4, 8)),
            pltpu.SemaphoreType.DMA((4, 4)),
            pltpu.SemaphoreType.DMA((4, 4)),
        ],
        compiler_params=pltpu.CompilerParams(
            collective_id=0, has_side_effects=True, vmem_limit_bytes=60 * 1024 * 1024
        ),
        name="train",
    )(
        offsets,
        counts.reshape(ROUNDS),
        embedding,
        adagrad.reshape(1, R_DEV),
        lhs_index,
        rhs_index,
        rel_ids,
        neg_index.reshape(ROUNDS, NEG),
        relation.T,
    )
    embedding_out, adagrad_out = pl.pallas_call(
        narrow,
        out_shape=[jax.ShapeDtypeStruct((R_DEV, D), F32), jax.ShapeDtypeStruct((1, R_DEV), F32)],
        in_specs=[vmem],
        out_specs=[vmem, vmem],
        name="narrow",
    )(state)
    return (embedding_out, adagrad_out.reshape(R_DEV))


def solution(mesh):
    return jax.shard_map(
        body,
        mesh=mesh,
        in_specs=(
            P(("dom", "row"), None),
            P(("dom", "row")),
            P(),
            P(),
            P(None, ("dom", "row")),
            P(None, ("dom", "row")),
            P(None, ("dom", "row")),
            P(None, ("dom", "row")),
            P(None, "dom", None),
        ),
        out_specs=(P(("dom", "row"), None), P(("dom", "row"))),
        check_vma=False,
    )
```

time: 157 us -> 120 us (0.76)
  Pallas kernels: 141 us -> 119 us
  local copies, waits for them, and re-layouts: 12.6 us -> 0 us
    pallas_call x1 -> x2, Pallas kernels: 141 us -> 119 us  [the longest x1 117 us: body(): pl.pallas_call(kernel, out_shape=jax.ShapeDtypeStruct((R_DEV, WIDE), F32)...]
    unnamed x3 -> x0, local copies, waits for them, and re-layouts: 8.26 us -> none
    slice x5 -> x0, local copies, waits for them, and re-layouts: 2.75 us -> none  [the longest x1 1.05 us: body(): embedding[:, :HALF]]
where the time goes in v2:
time: 120 us
  Pallas kernels  119 us (99%)
    pallas_call x1, Pallas kernels, body(): pl.pallas_call(kernel, out_shape=jax.ShapeDtypeStruct((R_DEV, WIDE), F32)...  117 us

profile of v2, /device:TPU:6, one launch (start us, length us, event | category | flops | bytes accessed | tf_op | source)
XLA Modules:
  0.0 119.8 jit_solution(11289972071256934380)
XLA Ops:
  0.6 117.5 %train.1.state = f32[64,512]{1,0:T(8,128)} custom-call(s32[2]{0:T(128)} %offsets.1, s32[2]{0:T(128)} %bitcast.7, f32[64,400]{1,0:T(8,128)} %embedding.1, f32[1,64]{1,0:T(1,128)} %bitcast.8, s32[2,2048]{1,0:T(2,128)} %lhs.1, s32[2,2048]{1,0:T(2,128)} %rhs.1, s32[2,2048]{1,0:T(2,128)} %rel.1, s32[2,128]{1,0:T(2,128)} %bitcast.6, bf16[400,4096]{1,0:T(8,128)(2,1)} %bitcast.5), custom_call_target="tpu_custom_call" | custom-call | tf_op jit(solution)/shard_map/train/pallas_call | solution.py:422
  118.1 1.7 %narrow.1 = (f32[64,400]{1,0:T(8,128)}, f32[1,64]{1,0:T(1,128)}) custom-call(f32[64,512]{1,0:T(8,128)} %train.1.state), custom_call_target="tpu_custom_call" | custom-call | tf_op jit(solution)/shard_map/narrow/pallas_call | solution.py:489

commit v3 on v2

--- a/solution.py
+++ b/solution.py
@@ -66,9 +66,9 @@
 
 
 def kernel(
-    offsets, counts, embedding, adagrad, lhs, rhs, rel, neg, relation,
+    offsets, counts, embedding_in, adagrad_in, lhs_in, rhs_in, rel_in, neg_in, relation,
     out,
-    raw, work0, state0, head0, home, home_t, rel_rows, hot_h, hot_t, hot_ht, hot_tt, query, tail_rows, pos_weights, neg_weights, grad_h, grad_t, neg_sum, neg_rows,
+    embedding, adagrad, lhs, rhs, rel, neg, raw, work0, state0, head0, home, home_t, rel_rows, hot_h, hot_t, hot_ht, hot_tt, query, tail_rows, pos_weights, neg_weights, grad_h, grad_t, neg_sum, neg_rows,
     state, work, stage, tail_in, head_in, shard_h, shard_t, panel_h, panel_t,
     acc_h, acc_t, near_h, near_t, far_send, far_h, far_t, row_send, got_h, got_t,
     raw_sem, a2a_send, a2a_recv, ag_send, ag_recv, rs_send, rs_recv,
@@ -81,13 +81,39 @@
 
     barrier = pltpu.get_barrier_semaphore()
 
-    def greet(j, c):
-        pl.semaphore_signal(barrier, inc=1, device_id=(lax.rem(me + j, ND), row), device_id_type=MESH)
-        return c
-
-    lax.fori_loop(1, ND, greet, 0)
+    def over_dom(act):
+        def step(i, c):
+            dz = NZ // 2 + (i + 1) // 2 * (1 - 2 * (i % 2))
+            for dy in (2, 1, 3, 0):
+                act(lax.rem(y + dy, NY) * NZ + lax.rem(z + dz, NZ))
+            return c
+
+        lax.fori_loop(0, NZ - 1, step, 0)
+        for dy in (2, 1, 3):
+            act(lax.rem(y + dy, NY) * NZ + z)
+
+    over_dom(lambda t: pl.semaphore_signal(barrier, inc=1, device_id=(t, row), device_id_type=MESH))
     for j in range(1, NR):
         pl.semaphore_signal(barrier, inc=1, device_id=(me, lax.rem(row + j, NR)), device_id_type=MESH)
+
+    fetches = [
+        pltpu.make_async_copy(src, dst, raw_sem.at[number])
+        for number, (src, dst) in enumerate(
+            [
+                (embedding_in, embedding),
+                (adagrad_in, adagrad),
+                (lhs_in, lhs),
+                (rhs_in, rhs),
+                (rel_in, rel),
+                (neg_in, neg),
+                (relation, raw),
+            ]
+        )
+    ]
+    for fetch in fetches:
+        fetch.start()
+    for fetch in fetches[:-1]:
+        fetch.wait()
 
     gap = jnp.zeros((R_DEV, 256 - HALF), F32)
     wide = jnp.concatenate([embedding[:, :HALF], gap, embedding[:, HALF:], gap], axis=1)
@@ -199,19 +225,10 @@
         acc_h[k, pl.ds(half * NX, NX)] = total.reshape(NX, R_DEV, WIDE)
 
     def spread(number, src, dst):
-        def send(dy, dz):
-            t = lax.rem(y + dy, NY) * NZ + lax.rem(z + dz, NZ)
+        def send(t):
             remote(src.at[t], dst.at[me], a2a_send.at[number], a2a_recv.at[number], (t, row)).start()
 
-        def step(i, c):
-            dz = NZ // 2 + (i + 1) // 2 * (1 - 2 * (i % 2))
-            for dy in (2, 1, 3, 0):
-                send(dy, dz)
-            return c
-
-        lax.fori_loop(0, NZ - 1, step, 0)
-        for dy in (2, 1, 3):
-            send(dy, 0)
+        over_dom(send)
         dst[me] = src[me]
 
     def spread_wait(number, src, dst):
@@ -226,7 +243,7 @@
             dst[j] = src[lax.rem(j + shift, ND)]
             return c
 
-        lax.fori_loop(0, ND, step, 0)
+        lax.fori_loop(0, ND, step, 0, unroll=8)
 
     def gather_far(number, src, panel):
         copies = []
@@ -283,8 +300,8 @@
             )
         return copies
 
-    def sum_near(number, acc, near, far):
-        near_copy(number, acc, near).wait()
+    def sum_near(copy, number, acc, near, far):
+        copy.wait()
         near[...] = near[...] + acc[pl.ds(core * NX, NX)]
         far_send[number] = near[...].astype(BF16)
         for copy in far_copies(number, far):
@@ -324,10 +341,8 @@
     def to_shard(value):
         return value.astype(F32).reshape(R_DEV, WIDE).astype(BF16)
 
-    fetch = pltpu.make_async_copy(relation, raw, raw_sem.at[0])
-    fetch.start()
     selectors(0)
-    fetch.wait()
+    fetches[-1].wait()
     relation_blocks(0, 0, 2)
 
     pl.semaphore_wait(barrier, ND - 1 + NR - 1)
@@ -360,30 +375,30 @@
             spread_wait(5, stage.at[1], tail_in.at[1])
             shard_t[1] = to_shard(tail_in[1])
             gather_start(3, shard_t.at[1], panel_t.at[1])
+            spread(7, state, home)
             gather_pass(2, shard_h, panel_h.at[1])
+            gather_pass(3, shard_t.at[1], panel_t.at[1])
             gather_end(2, shard_h, panel_h.at[1])
-            gather_pass(3, shard_t.at[1], panel_t.at[1])
             queries(1)
             gather_end(3, shard_t.at[1], panel_t.at[1])
+        near_tail, near_head = (near_copy(2 * k, acc_t.at[k], near_t.at[k]), near_copy(2 * k + 1, acc_h.at[k], near_h.at[k]))
         tail_grads(k)
-        tail_sums(k, 1 - core)
-        near_copy(2 * k, acc_t.at[k], near_t.at[k]).start()
-        tail_sums(k, core)
-        head_grads(k)
-        sum_near(2 * k, acc_t.at[k], near_t.at[k], far_t.at[k])
-        head_sums(k, 1 - core)
-        near_copy(2 * k + 1, acc_h.at[k], near_h.at[k]).start()
-        head_sums(k, core)
         if not last:
-            relation_blocks(1, 3, 4)
-        sum_near(2 * k + 1, acc_h.at[k], near_h.at[k], far_h.at[k])
-        row_send[2 * k] = to_rows(sum_far(2 * k, near_t.at[k], far_t.at[k]))
-        spread(2 + 4 * k, row_send.at[2 * k], got_t.at[k])
-        if not last:
-            relation_blocks(1, 4, 6)
+            head_grads(k)
+            tail_sums(k, 1 - core)
+            near_tail.start()
+            head_sums(k, 1 - core)
+            near_head.start()
+            tail_sums(k, core)
+            sum_near(near_tail, 2 * k, acc_t.at[k], near_t.at[k], far_t.at[k])
+            head_sums(k, core)
+            sum_near(near_head, 2 * k + 1, acc_h.at[k], near_h.at[k], far_h.at[k])
+            relation_blocks(1, 3, 5)
+            row_send[0] = to_rows(sum_far(0, near_t.at[0], far_t.at[0]))
+            spread(2, row_send.at[0], got_t.at[0])
             row_send[1] = to_rows(sum_far(1, near_h.at[0], far_h.at[0]))
             spread(3, row_send.at[1], got_h)
-            relation_blocks(1, 6, 8)
+            relation_blocks(1, 5, 8)
             selectors(1)
             spread_wait(9, state0, state)
             spread_wait(2, row_send.at[0], got_t.at[0])
@@ -393,8 +408,18 @@
             spread(4, work, head_in)
             rotated(1, work, stage.at[1], True)
             spread(5, stage.at[1], tail_in.at[1])
-            spread(7, state, home)
         else:
+            tail_sums(k, 1 - core)
+            near_tail.start()
+            tail_sums(k, core)
+            sum_near(near_tail, 2 * k, acc_t.at[k], near_t.at[k], far_t.at[k])
+            head_grads(k)
+            head_sums(k, 1 - core)
+            head_sums(k, core)
+            row_send[2] = to_rows(sum_far(2, near_t.at[1], far_t.at[1]))
+            spread(6, row_send.at[2], got_t.at[1])
+            near_head.start()
+            sum_near(near_head, 2 * k + 1, acc_h.at[k], near_h.at[k], far_h.at[k])
             head_sum = sum_far(2 * k + 1, near_h.at[k], far_h.at[k])
             spread_wait(7, state, home)
             spread_wait(6, row_send.at[2], got_t.at[1])
@@ -422,9 +447,15 @@
     state = pl.pallas_call(
         kernel,
         out_shape=jax.ShapeDtypeStruct((R_DEV, WIDE), F32),
-        in_specs=[smem, smem] + [vmem] * 6 + [pl.BlockSpec(memory_space=pl.ANY)],
+        in_specs=[smem, smem] + [pl.BlockSpec(memory_space=pl.ANY)] * 7,
         out_specs=vmem,
         scratch_shapes=[
+            V((R_DEV, D), F32),
+            V((1, R_DEV), F32),
+            V((ROUNDS, EDGES), jnp.int32),
+            V((ROUNDS, EDGES), jnp.int32),
+            V((ROUNDS, EDGES), jnp.int32),
+            V((ROUNDS, NEG), jnp.int32),
             V((D, NREL), BF16),
             V(rows, BF16),
             V(rows, F32),
@@ -463,7 +494,7 @@
             V((3,) + rows, BF16),
             V(rows, BF16),
             V((ROUNDS,) + rows, BF16),
-            pltpu.SemaphoreType.DMA((1,)),
+            pltpu.SemaphoreType.DMA((7,)),
             pltpu.SemaphoreType.DMA((10,)),
             pltpu.SemaphoreType.DMA((10,)),
             pltpu.SemaphoreType.DMA((4, 8)),

time: 120 us -> 117 us (0.975)
  Pallas kernels: 119 us -> 116 us
    pallas_call x1, Pallas kernels: 117 us -> 114 us  [body(): pl.pallas_call(kernel, out_shape=jax.ShapeDtypeStruct((R_DEV, WIDE), F32)...]
where the time goes in v3:
time: 117 us; the launch traced here: 116 us
  Pallas kernels  116 us (99%)
    pallas_call x1, Pallas kernels, body(): pl.pallas_call(kernel, out_shape=jax.ShapeDtypeStruct((R_DEV, WIDE), F32)...  114 us

profile of v3, /device:TPU:6, one launch (start us, length us, event | category | flops | bytes accessed | tf_op | source)
XLA Modules:
  0.0 116.2 jit_solution(10055957430435325898)
XLA Ops:
  0.6 113.9 %train.1.state = f32[64,512]{1,0:T(8,128)} custom-call(s32[2]{0:T(128)} %offsets.1, s32[2]{0:T(128)} %bitcast.7, f32[64,400]{1,0:T(8,128)} %embedding_in.1, f32[1,64]{1,0:T(1,128)} %bitcast.8, s32[2,2048]{1,0:T(2,128)} %lhs_in.1, s32[2,2048]{1,0:T(2,128)} %rhs_in.1, s32[2,2048]{1,0:T(2,128)} %rel_in.1, s32[2,128]{1,0:T(2,128)} %bitcast.6, ...), custom_call_target="tpu_custom_call" | custom-call | tf_op jit(solution)/shard_map/train/pallas_call | solution.py:447
  114.5 1.7 %narrow.1 = (f32[64,400]{1,0:T(8,128)}, f32[1,64]{1,0:T(1,128)}) custom-call(f32[64,512]{1,0:T(8,128)} %train.1.state), custom_call_target="tpu_custom_call" | custom-call | tf_op jit(solution)/shard_map/narrow/pallas_call | solution.py:520

commit v4 on v3

--- a/solution.py
+++ b/solution.py
@@ -231,9 +231,14 @@
         over_dom(send)
         dst[me] = src[me]
 
+    def spread_all(number, src, dst):
+        most = pl.ds(0, ND - 1)
+        return remote(
+            src.at[most], dst.at[most], a2a_send.at[number], a2a_recv.at[number], (lax.rem(me + 1, ND), row)
+        )
+
     def spread_wait(number, src, dst):
-        most = pl.ds(0, ND - 1)
-        remote(src.at[most], dst.at[most], a2a_send.at[number], a2a_recv.at[number], (lax.rem(me + 1, ND), row)).wait()
+        spread_all(number, src, dst).wait_recv()
 
     def rotated(k, src, dst, forward):
         by = offsets[k]
@@ -279,11 +284,13 @@
             onward.start()
 
     def gather_end(number, src, panel):
-        for copy in gather_far(number, src, panel):
+        gather_near(number, src, panel).wait_recv()
+        for copy in gather_passed(number, panel):
+            copy.wait_recv()
+
+    def gather_sent(number, src, panel):
+        for copy in gather_far(number, src, panel) + [gather_near(number, src, panel)] + gather_passed(number, panel):
             copy.wait_send()
-        gather_near(number, src, panel).wait()
-        for copy in gather_passed(number, panel):
-            copy.wait()
 
     def near_copy(number, acc, near):
         other = pl.ds((1 - core) * NX, NX)
@@ -301,7 +308,7 @@
         return copies
 
     def sum_near(copy, number, acc, near, far):
-        copy.wait()
+        copy.wait_recv()
         near[...] = near[...] + acc[pl.ds(core * NX, NX)]
         far_send[number] = near[...].astype(BF16)
         for copy in far_copies(number, far):
@@ -309,7 +316,7 @@
 
     def sum_far(number, near, far):
         for copy in far_copies(number, far):
-            copy.wait()
+            copy.wait_recv()
         return near[x] + (far[1].astype(F32) + far[2].astype(F32) + far[3].astype(F32))
 
     def is_sum():
@@ -348,13 +355,12 @@
     pl.semaphore_wait(barrier, ND - 1 + NR - 1)
     spread(0, work0, work)
     gather_start(0, head0, panel_h.at[0])
-    relation_blocks(0, 2, 5)
+    relation_blocks(0, 2, 6)
     gather_pass(0, head0, panel_h.at[0])
-    relation_blocks(0, 5, 7)
     spread_wait(0, work0, work)
     rotated(0, work, stage.at[0], True)
     spread(1, stage.at[0], tail_in.at[0])
-    relation_blocks(0, 7, 8)
+    relation_blocks(0, 6, 8)
     gather_end(0, head0, panel_h.at[0])
     queries(0)
     spread_wait(1, stage.at[0], tail_in.at[0])
@@ -427,6 +433,29 @@
             spread(8, stage.at[3], home_t)
             spread_wait(8, stage.at[3], home_t)
             finish(head_sum)
+
+    for number, src, dst in (
+        (0, work0, work),
+        (1, stage.at[0], tail_in.at[0]),
+        (2, row_send.at[0], got_t.at[0]),
+        (3, row_send.at[1], got_h),
+        (4, work, head_in),
+        (5, stage.at[1], tail_in.at[1]),
+        (6, row_send.at[2], got_t.at[1]),
+        (7, state, home),
+        (8, stage.at[3], home_t),
+        (9, state0, state),
+    ):
+        spread_all(number, src, dst).wait_send()
+    gather_sent(0, head0, panel_h.at[0])
+    gather_sent(1, shard_t.at[0], panel_t.at[0])
+    gather_sent(2, shard_h, panel_h.at[1])
+    gather_sent(3, shard_t.at[1], panel_t.at[1])
+    for k in range(ROUNDS):
+        for number, acc, near, far in ((2 * k, acc_t, near_t, far_t), (2 * k + 1, acc_h, near_h, far_h)):
+            near_copy(number, acc.at[k], near.at[k]).wait_send()
+            for copy in far_copies(number, far.at[k]):
+                copy.wait_send()
 
 
 def narrow(state, embedding_out, adagrad_out):

time: 117 us -> 117 us (level)
  no operation moved by 1% of the time
where the time goes in v4:
time: 117 us; the launch traced here: 116 us
  Pallas kernels  115 us (98%)
    pallas_call x1, Pallas kernels, body(): pl.pallas_call(kernel, out_shape=jax.ShapeDtypeStruct((R_DEV, WIDE), F32)...  114 us

profile of v4, /device:TPU:6, one launch (start us, length us, event | category | flops | bytes accessed | tf_op | source)
XLA Modules:
  0.0 116.0 jit_solution(516743069098516617)
XLA Ops:
  0.6 113.7 %train.1.state = f32[64,512]{1,0:T(8,128)} custom-call(s32[2]{0:T(128)} %offsets.1, s32[2]{0:T(128)} %bitcast.7, f32[64,400]{1,0:T(8,128)} %embedding_in.1, f32[1,64]{1,0:T(1,128)} %bitcast.8, s32[2,2048]{1,0:T(2,128)} %lhs_in.1, s32[2,2048]{1,0:T(2,128)} %rhs_in.1, s32[2,2048]{1,0:T(2,128)} %rel_in.1, s32[2,128]{1,0:T(2,128)} %bitcast.6, ...), custom_call_target="tpu_custom_call" | custom-call | tf_op jit(solution)/shard_map/train/pallas_call | solution.py:476
  114.4 1.7 %narrow.1 = (f32[64,400]{1,0:T(8,128)}, f32[1,64]{1,0:T(1,128)}) custom-call(f32[64,512]{1,0:T(8,128)} %train.1.state), custom_call_target="tpu_custom_call" | custom-call | tf_op jit(solution)/shard_map/narrow/pallas_call | solution.py:549
